TPU v7x, 768 devices: a whole 4x8x12 slice. The times are simulated.
768 devices in a mesh: dap: 24 (over x_lo, z), ctx: 32 (over y, x_hi, core).
Axes of the slice: x: 4 (x_hi: 2, x_lo: 2; x = x_hi * 2 + x_lo), y: 8, z: 12, core: 2. Of those that a mesh axis runs over, the one named last changes fastest.
Arguments:
- pair: bfloat16 [2304, 48, 128], P(('ctx', 'dap')), may hold values from -6 to 6
- cotangent: bfloat16 [2304, 48, 128], P(('ctx', 'dap')), may hold values from -6 to 6
- residue_mask: int32 [2304], replicated, may hold values 0 or 1
- bias: float32 [4, 2304, 2304], P(None, 'ctx'), may hold values from -250 to 250
- ln_attend: float32 [128], replicated, may hold values from 0.1 to 1.9
- w_in: bfloat16 [128, 512], replicated, may hold values from -0.5 to 0.5
- w_out: bfloat16 [128, 128], replicated, may hold values from -0.5 to 0.5
- ln_trans: float32 [128], replicated, may hold values from 0.1 to 1.9
- w_up: bfloat16 [128, 512], replicated, may hold values from -0.5 to 0.5
- w_down: bfloat16 [512, 128], replicated, may hold values from -0.25 to 0.25
Outputs:
- pair_grad: float32 [2304, 48, 128], P(('ctx', 'dap'))
- bias_grad: float32 [4, 2304, 2304], P(None, 'ctx', 'dap')
All inputs are finite; a program needn't handle non-finite values.
Results may differ from a plain program's by a relative error of at most 0.01.
Values may be sent and summed in bfloat16 or wider, within the bound.
No kernel may reach another device: no remote copies, remote signals or barrier semaphores. Data moves between devices by JAX's collectives and lax.ppermute only.
A program may use at most 64 MiB of HBM per device.

v0:
```python
from functools import partial

import jax
import jax.numpy as jnp
from jax import lax
from jax.sharding import PartitionSpec as P

H = 4
DH = 32


def layer_norm(inputs, gain):
    average = jnp.mean(inputs, axis=-1, keepdims=True)
    centred = inputs - average
    variance = jnp.mean(centred * centred, axis=-1, keepdims=True)
    return centred * lax.rsqrt(variance + 1e-05) * gain


def flat_dot(inputs, weight):
    leading = inputs.shape[:-1]
    result = jnp.dot(
        inputs.reshape(-1, inputs.shape[-1]), weight, preferred_element_type=jnp.float32
    )
    return result.reshape(leading + (weight.shape[1],))


def exact_dot(inputs, weight):
    leading = inputs.shape[:-1]
    result = jnp.dot(
        inputs.reshape(-1, inputs.shape[-1]),
        weight,
        preferred_element_type=jnp.float32,
        precision=lax.Precision.HIGHEST,
    )
    return result.reshape(leading + (weight.shape[1],))


def mix(pattern, first_op, second_op):
    return jnp.einsum(pattern, first_op, second_op, preferred_element_type=jnp.float32)


def split_heads(tensor):
    return tensor.reshape(tensor.shape[0], tensor.shape[1], H, DH)


def merge_heads(tensor):
    return tensor.reshape(tensor.shape[0], tensor.shape[1], H * DH)


def attend_forward(queries, keys_all, values_all, bias_rows, key_bias):
    scale = DH ** (-0.5)
    scores = mix("ijhd,kjhd->hijk", split_heads(queries), split_heads(keys_all)) * scale
    scores = scores + bias_rows[:, :, None, :] + key_bias
    row_max = jnp.max(scores, axis=-1, keepdims=True)
    exponent = jnp.exp(scores - row_max)
    weights = exponent / jnp.sum(exponent, axis=-1, keepdims=True)
    weights_b = weights.astype(jnp.bfloat16)
    heads_out = merge_heads(mix("hijk,kjhd->ijhd", weights_b, split_heads(values_all)))
    return (weights, weights_b, heads_out)


def attend_backward(queries, keys_all, values_all, weights, weights_b, d_heads):
    scale = DH ** (-0.5)
    d_heads_b = split_heads(d_heads.astype(jnp.bfloat16))
    d_weights = mix("ijhd,kjhd->hijk", d_heads_b, split_heads(values_all))
    row_dot = jnp.sum(weights * d_weights, axis=-1, keepdims=True)
    d_scores = weights * (d_weights - row_dot)
    d_scores_b = d_scores.astype(jnp.bfloat16)
    d_query = merge_heads(mix("hijk,kjhd->ijhd", d_scores_b, split_heads(keys_all))) * scale
    d_key = merge_heads(mix("hijk,ijhd->kjhd", d_scores_b, split_heads(queries))) * scale
    d_value = merge_heads(mix("hijk,ijhd->kjhd", weights_b, d_heads_b))
    d_bias = jnp.sum(d_scores, axis=2)
    return (d_query, d_key, d_value, d_bias)


def transition_back(residual_mid, cotangent_cols, ln_trans, w_up, w_down):
    trans_in, trans_back = jax.vjp(partial(layer_norm, gain=ln_trans), residual_mid)
    pre_act = flat_dot(trans_in.astype(jnp.bfloat16), w_up)
    gate_s = jax.nn.sigmoid(pre_act)
    slope = gate_s + pre_act * gate_s * (1.0 - gate_s)
    d_hidden = (flat_dot(cotangent_cols, w_down.T) * slope).astype(jnp.bfloat16)
    d_trans = flat_dot(d_hidden, w_up.T)
    return cotangent_cols.astype(jnp.float32) + trans_back(d_trans)[0]


def per_device(pair, cotangent, residue_mask, bias, ln_attend, w_in, w_out, ln_trans, w_up, w_down):
    inner_width = H * DH
    column_pair, column_cot = (
        lax.all_to_all(pair, "dap", split_axis=1, concat_axis=0, tiled=True),
        lax.all_to_all(cotangent, "dap", split_axis=1, concat_axis=0, tiled=True),
    )
    source = column_pair.astype(jnp.float32)
    normed, norm_back = jax.vjp(partial(layer_norm, gain=ln_attend), source)
    projected = flat_dot(normed.astype(jnp.bfloat16), w_in)
    queries = projected[..., :inner_width].astype(jnp.bfloat16)
    keys_local = projected[..., inner_width : 2 * inner_width].astype(jnp.bfloat16)
    values_local = projected[..., 2 * inner_width : 3 * inner_width].astype(jnp.bfloat16)
    gate_raw = projected[..., 3 * inner_width :]
    keys_all, values_all = (
        lax.all_gather(keys_local, "ctx", axis=0, tiled=True),
        lax.all_gather(values_local, "ctx", axis=0, tiled=True),
    )
    live_keys = residue_mask.astype(jnp.float32)
    key_bias = (live_keys - 1.0) * 1000000000.0
    weights, weights_b, heads_out = attend_forward(queries, keys_all, values_all, bias, key_bias)
    gate_open = jax.nn.sigmoid(gate_raw)
    gated = (heads_out * gate_open).astype(jnp.bfloat16)
    residual_mid = source + flat_dot(gated, w_out)
    d_mid = transition_back(residual_mid, column_cot, ln_trans, w_up, w_down)
    d_gated = flat_dot(d_mid.astype(jnp.bfloat16), w_out.T)
    d_heads = d_gated * gate_open
    d_gate = d_gated * heads_out * gate_open * (1.0 - gate_open)
    d_query, d_key, d_value, d_bias = attend_backward(
        queries, keys_all, values_all, weights, weights_b, d_heads
    )
    bias_share = lax.psum_scatter(d_bias, "dap", scatter_dimension=2, tiled=True)
    w_full = w_in.astype(jnp.float32)
    w_key = w_full[:, inner_width : 2 * inner_width].T
    w_value = w_full[:, 2 * inner_width : 3 * inner_width].T
    local_part = exact_dot(d_query, w_full[:, :inner_width].T) + exact_dot(
        d_gate, w_full[:, 3 * inner_width :].T
    )
    key_sum, value_sum = (
        lax.psum_scatter(d_key, "ctx", scatter_dimension=0, tiled=True),
        lax.psum_scatter(d_value, "ctx", scatter_dimension=0, tiled=True),
    )
    remote_part = exact_dot(key_sum, w_key) + exact_dot(value_sum, w_value)
    d_normed = local_part + remote_part
    d_pair = d_mid + norm_back(d_normed)[0]
    pair_grad = lax.all_to_all(d_pair, "dap", split_axis=0, concat_axis=1, tiled=True)
    return (pair_grad, bias_share)


def solution(mesh):
    in_specs = (
        P(("ctx", "dap"), None, None),
        P(("ctx", "dap"), None, None),
        P(),
        P(None, "ctx", None),
        P(),
        P(),
        P(),
        P(),
        P(),
        P(),
    )
    out_specs = (P(("ctx", "dap"), None, None), P(None, "ctx", "dap"))
    return jax.shard_map(
        per_device, mesh=mesh, in_specs=in_specs, out_specs=out_specs, check_vma=False
    )
```

profile of v0, /device:TPU:16, one launch (start us, length us, event | category | flops | bytes accessed | tf_op | source)
XLA Modules:
  0.0 639.7 jit_solution(1353658219518526162)
XLA Ops:
  7.2 0.8 copy.114
  8.0 26.9 %all_to_all.45 = bf16[3,48,128]{2,0,1:T(4,128)(2,1)S(1)} all-to-all(bf16[3,48,128]{2,0,1:T(4,128)(2,1)S(1)} %copy.114), channel_id=1, replica_groups=mesh['dap'=24,'ctx'=32] {'dap'}, dimensions={1} | all-to-all | bytes 73728 | tf_op jit(solution)/shard_map/all_to_all | solution.py:89
  35.1 0.3 copy.117
  35.5 0.3 fusion.47
  35.8 0.3 copy.121
  36.2 1.2 fusion.98
  37.3 0.6 fusion.97
  38.0 0.7 all-gather.3.cloned.1.call-update
  38.7 1.4 copy.110
  40.2 3.8 all-to-all-start
  44.0 0.7 add_multiply_fusion
  44.7 10.0 %all-to-all-done = bf16[3,48,128]{2,0,1:T(4,128)(2,1)S(1)} async-done(((bf16[3,48,128]{2,0,1:T(4,128)(2,1)}), bf16[3,48,128]{2,0,1:T(4,128)(2,1)S(1)}, u32[]{:S(2)}, u32[]{:S(2)}) %all-to-all-start) | async-done | bytes 36896 | tf_op jit(solution)/shard_map/all_to_all | solution.py:90
  55.0 65.9 %all-gather.5.cloned.1.call-done = bf16[2304,2,128]{2,0,1:T(8,128)(2,1)} async-done(((bf16[72,2,128]{2,0,1:T(8,128)(2,1)}), bf16[2304,2,128]{2,0,1:T(8,128)(2,1)}) %all-gather.5.cloned.1.call-update) | async-done | bytes 1179664 | tf_op jit(solution)/shard_map/all_gather | solution.py:100
  120.9 1.6 copy.123
  122.4 6.3 fusion.99
  128.7 3.1 fusion.94
  131.8 78.8 %all-gather.3.cloned.1.call-done = bf16[2304,2,128]{2,0,1:T(8,128)(2,1)} async-done(((bf16[72,2,128]{2,0,1:T(8,128)(2,1)}), bf16[2304,2,128]{2,0,1:T(8,128)(2,1)}) %all-gather.3.cloned.1.call-update) | async-done | bytes 1179664 | tf_op jit(solution)/shard_map/all_gather | solution.py:101
  210.6 2.4 copy.122
  213.0 2.1 fusion.12
  215.2 0.3 fusion.104
  215.5 0.2 multiply_reduce_fusion.2
  215.7 1.0 fusion.37
  216.6 2.0 multiply_reduce_fusion.1
  218.7 1.1 fusion.95
  219.8 1.6 multiply_convert_fusion
  221.6 2.2 fusion.14
  223.7 11.1 %fusion.96 = (f32[4,72,2304]{2,1,0:T(8,128)}, bf16[4,72,2,2304]{3,1,2,0:T(8,128)(2,1)}) fusion(f32[4,2,2304,72]{2,3,1,0:T(8,128)S(1)} %fusion.14, f32[4,72,2,2304]{3,1,2,0:T(8,128)} %get-tuple-element.14, f32[4,72,2]{1,2,0:T(2,128)S(1)} %get-tuple-element.13), kind=kOutput, calls=%fused_computation.115 | output fusion | flops 8629055 | bytes 15927552 | tf_op jit(solution)/shard_map/sub | solution.py:67
  234.9 3.7 convolution_multiply_fusion
  238.6 3.1 copy.137
  241.8 2.0 fusion.10
  243.7 3.2 copy.139
  246.9 0.2 reduce-scatter.10.cloned.1.call-start
  247.2 4.0 copy.143
  251.2 5.7 reshape.187
  256.9 1.8 copy-done.1
  258.7 2.1 fusion.19
  260.9 0.3 fusion.76
  261.1 0.2 convolution_add_fusion.1
  261.4 113.8 %reduce-scatter.6.cloned.1.call-done = f32[72,2,128]{2,0,1:T(8,128)} async-done(((f32[2304,2,128]{2,0,1:T(8,128)}), f32[72,2,128]{2,0,1:T(8,128)}) %reduce-scatter.6.cloned.1.call-update) | async-done | bytes 73744 | tf_op jit(solution)/shard_map/reduce_scatter | solution.py:124
  375.2 1.1 fusion.73
  376.3 139.3 %reduce-scatter.8.cloned.1.call-done = f32[72,2,128]{2,0,1:T(8,128)} async-done(((f32[2304,2,128]{2,0,1:T(8,128)}), f32[72,2,128]{2,0,1:T(8,128)}) %reduce-scatter.8.cloned.1.call-update) | async-done | bytes 73744 | tf_op jit(solution)/shard_map/reduce_scatter | solution.py:125
  515.6 1.2 multiply_reduce_fusion
  516.8 0.2 fusion.87
  517.3 21.0 %all_to_all.46 = f32[72,2,128]{2,1,0:T(2,128)S(1)} all-to-all(f32[72,2,128]{2,1,0:T(2,128)S(1)} %copy.140), channel_id=1, replica_groups=mesh['dap'=24,'ctx'=32] {'dap'}, dimensions={0} | all-to-all | bytes 147456 | tf_op jit(solution)/shard_map/all_to_all | solution.py:130
  538.2 0.7 copy.141
  538.9 92.4 %reduce-scatter.10.cloned.1.call-done = f32[96,288]{1,0:T(8,128)} async-done(((f32[2304,288]{1,0:T(8,128)}), f32[96,288]{1,0:T(8,128)}) %reduce-scatter.10.cloned.1.call-update) | async-done | bytes 110608
  631.3 1.1 reshape.188
  632.4 0.8 copy.144
  (43 shorter events, 1.3 us)
Async XLA Ops:
  7.2 208.5 %copy-start = (bf16[128,512]{1,0:T(8,128)(2,1)S(1)}, bf16[128,512]{1,0:T(8,128)(2,1)}, u32[]{:S(2)}) copy-start(bf16[128,512]{1,0:T(8,128)(2,1)} %param.18) | copy-start | bytes 393220
  7.2 113.7 %all-gather.5.cloned.1.call-start = ((), (), s32[]{:S(2)}) async-start(), calls=%async_computation.7 | async-start | bytes 1216512 | tf_op jit(solution)/shard_map/all_gather | solution.py:100
  38.0 172.6 %all-gather.3.cloned.1.call-start = ((), (), s32[]{:S(2)}) async-start(), calls=%async_computation.6 | async-start | bytes 1216512 | tf_op jit(solution)/shard_map/all_gather | solution.py:101
  40.2 14.6 %all-to-all-start = ((bf16[3,48,128]{2,0,1:T(4,128)(2,1)}), bf16[3,48,128]{2,0,1:T(4,128)(2,1)S(1)}, u32[]{:S(2)}, u32[]{:S(2)}) async-start(bf16[3,48,128]{2,0,1:T(4,128)(2,1)} %copy.110), calls=%async_computation | async-start | bytes 98304 | tf_op jit(solution)/shard_map/all_to_all | solution.py:90
  44.0 331.2 %reduce-scatter.6.cloned.1.call-start = ((), (), s32[]{:S(2)}) async-start(), calls=%async_computation.8 | async-start | bytes 2433024 | tf_op jit(solution)/shard_map/reduce_scatter | solution.py:124
  122.4 6.3 copy-start.3
  213.0 2.2 copy-start.7
  213.0 2.7 copy-start.6
  241.7 273.9 %reduce-scatter.8.cloned.1.call-start = ((), (), s32[]{:S(2)}) async-start(), calls=%async_computation.9 | async-start | bytes 2433024 | tf_op jit(solution)/shard_map/reduce_scatter | solution.py:125
  243.7 3.4 copy-start.2
  246.9 384.4 %reduce-scatter.10.cloned.1.call-start = ((), (), s32[]{:S(2)}) async-start(), calls=%async_computation.10 | async-start | bytes 3686400
  256.9 1.8 copy-start.1
  258.7 2.2 copy-start.4
  258.7 2.4 copy-start.8
  258.7 256.9 %copy-start.5 = (f32[128]{0:T(128)S(1)}, f32[128]{0:T(128)}, u32[]{:S(2)}) copy-start(f32[128]{0:T(128)} %param.14) | copy-start | bytes 1540
Sparse Core Ops, SparseCore 0:
  38.1 82.6 all-gather.4
  124.7 85.8 all-gather.2
  241.8 133.3 reduce-scatter.5
  381.3 134.2 reduce-scatter.7
  518.6 112.7 reduce-scatter.9
where the time goes:
time: 641 us; the launch traced here: 640 us
  waiting for transfers between devices  501 us (78%)
  blocking collectives  47.9 us (7%)
  local copies, waits for them, and re-layouts  28.2 us (4%)
  matrix products  27.2 us (4%)
  other arithmetic  17.2 us (3%)
  between operations  14 us (2%)
    reduce_scatter x1, waiting for transfers between devices, per_device(): lax.psum_scatter(d_value, 'ctx', scatter_dimension=0, tiled=True)  139 us
    reduce_scatter x1, waiting for transfers between devices, per_device(): lax.psum_scatter(d_key, 'ctx', scatter_dimension=0, tiled=True)  114 us
    unnamed x6, waiting for transfers between devices  93.2 us
    all_gather x1, waiting for transfers between devices, per_device(): lax.all_gather(values_local, 'ctx', axis=0, tiled=True)  78.8 us
    all_gather x1, waiting for transfers between devices, per_device(): lax.all_gather(keys_local, 'ctx', axis=0, tiled=True)  65.9 us
    all_to_all x1, blocking collectives, per_device(): lax.all_to_all(pair, 'dap', split_axis=1, concat_axis=0, tiled=True)  26.9 us
    all_to_all x1, blocking collectives, per_device(): lax.all_to_all(d_pair, 'dap', split_axis=0, concat_axis=1, tiled=True)  21 us
    unnamed x24, local copies, waits for them, and re-layouts  15.6 us
  transfers between devices with their start and end apart: 6, of which 6 were waited for; matrix products, arithmetic and copies ran while one was open for 5% of the time, Pallas kernels for 0%

commit v1 on v0

v1 whole, which is shorter than its diff:
```python
import numpy as np

import jax
import jax.numpy as jnp
from jax import lax
from jax.experimental import pallas as pl
from jax.experimental.pallas import tpu as pltpu
from jax.sharding import PartitionSpec as P

C = 128
H = 4
DH = 32
SCALE = DH ** (-0.5)
F32 = jnp.float32
BF16 = jnp.bfloat16

CORES = [[2 * m, 2 * m + 1] for m in range(16)]
CHIPS = [[2 * m + r for m in range(16)] for r in range(2)]


def mm(a, b):
    return jnp.dot(a, b, preferred_element_type=F32)


def mm_t(a, b):
    return lax.dot_general(a, b, (((1,), (1,)), ((), ())), preferred_element_type=F32)


def halves(x):
    hi = x.astype(BF16)
    return hi, (x - hi.astype(F32)).astype(BF16)


def center(x):
    mean = jnp.mean(x, axis=-1, keepdims=True)
    cen = x - mean
    var = jnp.mean(cen * cen, axis=-1, keepdims=True)
    rstd = lax.rsqrt(var + 1e-05)
    return cen * rstd, rstd


def center_back(hat, rstd, gain, d_out):
    t = d_out * gain
    a = jnp.mean(t, axis=-1, keepdims=True)
    b = jnp.mean(t * hat, axis=-1, keepdims=True)
    return rstd * (t - a - hat * b)


def prep_kernel(x_ref, order_ref, gain_ref, normed_ref, both_ref):
    both = mm(order_ref[...], x_ref[...])
    both_ref[...] = both
    hat, _ = center(both[: both.shape[0] // 2])
    normed_ref[...] = (hat * gain_ref[...]).astype(BF16)


def main_kernel(
    g_ref, normed_ref, both_ref, bias_ref, mask_ref, w_in_ref, w_out_ref, gain_ref, w_up_ref, w_down_ref,
    db_ref, dn_ref, loc_ref,
    k_scr, v_scr, s_scr, w_scr, wb_scr, ds_scr, dsb_scr, dn_scr,
):
    n = bias_ref.shape[1]
    rows = bias_ref.shape[0] // H
    cols = 2

    def make_kv(p, _):
        parts = []
        for core in range(2):
            start = pl.multiple_of((core * (n // (2 * rows)) + p) * (cols * rows), cols * rows)
            x = g_ref[pl.ds(start, cols * rows), :]
            parts.append(mm(x, w_in_ref[:, C : 3 * C]))
        dest = pl.multiple_of(p * 2 * rows, 2 * rows)
        for j in range(cols):
            kv = jnp.concatenate([q[j * rows : (j + 1) * rows] for q in parts], axis=0).astype(BF16)
            k_scr[j, pl.ds(dest, 2 * rows), :] = kv[:, :C]
            v_scr[j, pl.ds(dest, 2 * rows), :] = kv[:, C:]
        return 0

    lax.fori_loop(0, n // (2 * rows), make_kv, 0)

    normed = normed_ref[...]
    queries = mm(normed, w_in_ref[:, :C])
    gate_raw = mm(normed, w_in_ref[:, 3 * C :])
    key_bias = (mask_ref[...].astype(F32) - 1.0) * 1000000000.0

    def head_mask(h):
        lane = lax.broadcasted_iota(jnp.int32, (rows, C), 1)
        return (lane >= h * DH) & (lane < (h + 1) * DH)

    def stack(x):
        return jnp.concatenate([jnp.where(head_mask(h), x, 0.0) for h in range(H)], axis=0).astype(BF16)

    def unstack(x):
        out = jnp.where(head_mask(0), x[:rows], 0.0)
        for h in range(1, H):
            out = jnp.where(head_mask(h), x[h * rows : (h + 1) * rows], out)
        return out

    q_stack = [stack(queries[j * rows : (j + 1) * rows]) for j in range(cols)]
    heads = []
    for j in range(cols):
        s_scr[...] = mm_t(q_stack[j], k_scr[j])

        def soft(r, _, j=j):
            at = pl.ds(pl.multiple_of(r * 16, 16), 16)
            s = s_scr[at, :] * SCALE + bias_ref[at, :] + key_bias
            e = jnp.exp(s - jnp.max(s, axis=-1, keepdims=True))
            w = e * (1.0 / jnp.sum(e, axis=-1, keepdims=True))
            w_scr[j, at, :] = w
            wb_scr[j, at, :] = w.astype(BF16)
            return 0

        lax.fori_loop(0, H * rows // 16, soft, 0, unroll=2)
        heads.append(unstack(mm(wb_scr[j], v_scr[j])))
    heads_out = jnp.concatenate(heads, axis=0)

    open_ = jax.nn.sigmoid(gate_raw)
    both = both_ref[...]
    source, cot = both[: cols * rows], both[cols * rows :]
    gated = (heads_out * open_).astype(BF16)
    mid = source + mm(gated, w_out_ref[...])
    mid_hat, mid_rstd = center(mid)
    gain = gain_ref[...]
    pre = mm((mid_hat * gain).astype(BF16), w_up_ref[...])
    gs = jax.nn.sigmoid(pre)
    slope = gs + pre * gs * (1.0 - gs)
    d_hidden = (mm_t(cot.astype(BF16), w_down_ref[...]) * slope).astype(BF16)
    d_trans = mm_t(d_hidden, w_up_ref[...])
    d_mid = cot + center_back(mid_hat, mid_rstd, gain, d_trans)
    d_gated = mm_t(d_mid.astype(BF16), w_out_ref[...])
    d_heads = d_gated * open_
    d_gate = d_gated * heads_out * open_ * (1.0 - open_)
    loc_ref[: cols * rows, :] = d_mid

    w_kv = w_in_ref[:, C : 3 * C]
    d_query = []
    for j in range(cols):
        do_stack = stack(d_heads[j * rows : (j + 1) * rows])
        s_scr[...] = mm_t(do_stack, v_scr[j])

        def back(r, _, j=j):
            at = pl.ds(pl.multiple_of(r * 16, 16), 16)
            w = w_scr[j, at, :]
            dw = s_scr[at, :]
            ds = w * (dw - jnp.sum(w * dw, axis=-1, keepdims=True))
            dsb_scr[at, :] = ds.astype(BF16)
            if j == 0:
                ds_scr[at, :] = ds
            else:
                ds_scr[at, :] = ds_scr[at, :] + ds
            return 0

        lax.fori_loop(0, H * rows // 16, back, 0, unroll=2)
        ds_b = dsb_scr[...]
        d_query.append(unstack(mm(ds_b, k_scr[j])) * SCALE)
        dk = mm(q_stack[j].astype(F32).T.astype(BF16), ds_b) * SCALE
        dv = mm(do_stack.astype(F32).T.astype(BF16), wb_scr[j])
        hi, lo = halves(jnp.concatenate([dk, dv], axis=0))
        dn_scr[j] = (mm(w_kv, hi) + mm(w_kv, lo)).T

    hi, lo = halves(jnp.concatenate([jnp.concatenate(d_query, axis=0), d_gate], axis=1))
    w_qg = jnp.concatenate([w_in_ref[:, :C], w_in_ref[:, 3 * C :]], axis=1)
    loc_ref[cols * rows :, :] = mm_t(hi, w_qg) + mm_t(lo, w_qg)

    def put_dn(p, _):
        for core in range(2):
            at = pl.multiple_of((2 * p + core) * rows, rows)
            block = jnp.concatenate([dn_scr[j, pl.ds(at, rows), :] for j in range(cols)], axis=0)
            start = pl.multiple_of((core * (n // (2 * rows)) + p) * (cols * rows), cols * rows)
            dn_ref[pl.ds(start, cols * rows), :] = block.astype(BF16)
        return 0

    lax.fori_loop(0, n // (2 * rows), put_dn, 0)

    def put_db(t, _):
        at = pl.ds(pl.multiple_of(t * C, C), C)
        xs = [ds_scr[pl.ds(h * rows, rows), at] for h in range(H)]
        groups = []
        for a in range(4):
            out = xs[a]
            for h in range(H):
                if h != a:
                    out = jnp.where(head_mask(h), pltpu.roll(xs[h], ((h - a) * DH) % C, 1), out)
            groups.append(out)
        start = pl.multiple_of(t * 4 * rows, 4 * rows)
        db_ref[pl.ds(start, 4 * rows), :] = jnp.concatenate(groups, axis=0).astype(BF16)
        return 0

    lax.fori_loop(0, n // C, put_db, 0)


def last_kernel(parts_ref, loc_ref, both_ref, gain_ref, order_ref, out_ref):
    half = loc_ref.shape[0] // 2
    total = loc_ref[half:, :]
    for p in range(parts_ref.shape[0]):
        total = total + parts_ref[p].astype(F32)
    hat, rstd = center(both_ref[:half, :])
    d_pair = loc_ref[:half, :] + center_back(hat, rstd, gain_ref[...], total)
    out_ref[...] = mm(order_ref[...], d_pair.astype(BF16)).astype(BF16)


def bias_kernel(parts_ref, out_ref):
    rows = out_ref.shape[1]
    total = parts_ref[0].astype(F32)
    for p in range(1, parts_ref.shape[0]):
        total = total + parts_ref[p].astype(F32)
    for h in range(H):
        out_ref[h] = jnp.concatenate(
            [total[t * rows : (t + 1) * rows, h * DH : (h + 1) * DH] for t in range(3)], axis=1
        )


def call(kernel, out_shape, scratch=(), limit=48):
    return pl.pallas_call(
        kernel,
        out_shape=out_shape,
        scratch_shapes=list(scratch),
        compiler_params=pltpu.CompilerParams(vmem_limit_bytes=limit * 1024 * 1024),
    )


def one_hot(source_of):
    out = np.zeros((len(source_of), len(source_of)), np.float32)
    out[np.arange(len(source_of)), source_of] = 1.0
    return out


def per_device(pair, cotangent, residue_mask, bias, ln_attend, w_in, w_out, ln_trans, w_up, w_down):
    n_dap = lax.axis_size("dap")
    n_ctx = lax.axis_size("ctx")
    local, n_cols, _ = pair.shape
    cols = n_cols // n_dap
    rows = local * n_dap
    n = rows * n_ctx
    block = cols * rows
    each = cols * local

    both = jnp.stack([pair, cotangent]).reshape(2, local, n_dap, cols, C)
    both = both.transpose(2, 0, 3, 1, 4).reshape(n_dap * 2 * each, C)
    both = lax.all_to_all(both, "dap", 0, 0, tiled=True)
    source_of = [
        (i // local) * 2 * each + a * each + j * local + i % local
        for a in range(2)
        for j in range(cols)
        for i in range(rows)
    ]
    normed, both = call(
        prep_kernel,
        (jax.ShapeDtypeStruct((block, C), BF16), jax.ShapeDtypeStruct((2 * block, C), F32)),
    )(both, jnp.asarray(one_hot(source_of), BF16), ln_attend[None])

    gathered = normed
    gathered = jnp.broadcast_to(gathered[None], (16, block, C)).reshape(16 * block, C)
    gathered = lax.all_to_all(gathered, "ctx", 0, 0, tiled=True, axis_index_groups=CHIPS)
    other = lax.ppermute(gathered, "ctx", [(i, i ^ 1) for i in range(n_ctx)])
    first = lax.axis_index("ctx") % 2 == 0
    gathered = jnp.concatenate([jnp.where(first, gathered, other), jnp.where(first, other, gathered)], axis=0)

    db, dn, loc = call(
        main_kernel,
        (
            jax.ShapeDtypeStruct((n // DH * rows, C), BF16),
            jax.ShapeDtypeStruct((n * cols, C), BF16),
            jax.ShapeDtypeStruct((2 * block, C), F32),
        ),
        scratch=(
            pltpu.VMEM((cols, n, C), BF16),
            pltpu.VMEM((cols, n, C), BF16),
            pltpu.VMEM((H * rows, n), F32),
            pltpu.VMEM((cols, H * rows, n), F32),
            pltpu.VMEM((cols, H * rows, n), BF16),
            pltpu.VMEM((H * rows, n), F32),
            pltpu.VMEM((H * rows, n), BF16),
            pltpu.VMEM((cols, n, C), F32),
        ),
        limit=56,
    )(
        gathered, normed, both, bias.reshape(H * rows, n), residue_mask[None], w_in, w_out, ln_trans[None],
        w_up, w_down,
    )

    db = lax.all_to_all(db, "dap", 0, 0, tiled=True).reshape(n_dap, n // n_dap // DH * rows, C)
    bias_grad = call(bias_kernel, jax.ShapeDtypeStruct((H, rows, n // n_dap), F32))(db)

    dn = lax.all_to_all(dn, "ctx", 0, 0, tiled=True, axis_index_groups=CORES)
    dn = dn.reshape(2, 16 * block, C).astype(F32).sum(0).astype(BF16)
    dn = lax.all_to_all(dn, "ctx", 0, 0, tiled=True, axis_index_groups=CHIPS).reshape(16, block, C)

    back_of = [
        j * rows + d * local + r for d in range(n_dap) for r in range(local) for j in range(cols)
    ]
    d_pair = call(last_kernel, jax.ShapeDtypeStruct((block, C), BF16))(
        dn, loc, both, ln_attend[None], jnp.asarray(one_hot(back_of), BF16)
    )
    d_pair = lax.all_to_all(d_pair, "dap", 0, 0, tiled=True).reshape(n_dap, local, cols, C)
    pair_grad = d_pair.transpose(1, 0, 2, 3).reshape(local, n_cols, C).astype(F32)
    return (pair_grad, bias_grad)


def solution(mesh):
    in_specs = (
        P(("ctx", "dap"), None, None),
        P(("ctx", "dap"), None, None),
        P(),
        P(None, "ctx", None),
        P(),
        P(),
        P(),
        P(),
        P(),
        P(),
    )
    out_specs = (P(("ctx", "dap"), None, None), P(None, "ctx", "dap"))
    return jax.shard_map(
        per_device, mesh=mesh, in_specs=in_specs, out_specs=out_specs, check_vma=False
    )
```

time: 641 us -> 186 us (0.29)
  the two profiles are of different devices: /device:TPU:16 before, /device:TPU:2 now
where the time goes in v1:
time: 186 us; the launch traced here: 185 us
  blocking collectives  101 us (54%)
  waiting for transfers between devices  46.1 us (25%)
  Pallas kernels  24.8 us (13%)
  starting transfers between devices  6.77 us (4%)
  local copies, waits for them, and re-layouts  3.71 us (2%)
  other arithmetic  2.69 us (1%)
    all_to_all x1, waiting for transfers between devices, per_device(): lax.all_to_all(db, 'dap', 0, 0, tiled=True)  44.7 us
    all_to_all x1, blocking collectives, per_device(): lax.all_to_all(gathered, 'ctx', 0, 0, tiled=True, axis_index_groups=CHIPS)  28.1 us
    all_to_all x1, blocking collectives, per_device(): both = lax.all_to_all(both, 'dap', 0, 0, tiled=True)  26.8 us
    all_to_all x1, blocking collectives, per_device(): lax.all_to_all(dn, 'ctx', 0, 0, tiled=True, axis_index_groups=CHIPS)  24.3 us
    pallas_call x1, Pallas kernels, per_device(): call(main_kernel, (jax.ShapeDtypeStruct((n // DH * rows, C), BF16), jax.S...  23.1 us
    all_to_all x1, blocking collectives, per_device(): lax.all_to_all(d_pair, 'dap', 0, 0, tiled=True)  15.6 us
    all_to_all x1, blocking collectives, per_device(): dn = lax.all_to_all(dn, 'ctx', 0, 0, tiled=True, axis_index_groups=CORES)  5.8 us
    all_to_all x1, starting transfers between devices, per_device(): lax.all_to_all(db, 'dap', 0, 0, tiled=True)  4.86 us
  transfers between devices with their start and end apart: 2, of which 2 were waited for; matrix products, arithmetic and copies ran while one was open for 1% of the time, Pallas kernels for 0%

profile of v1, /device:TPU:2, one launch (start us, length us, event | category | flops | bytes accessed | tf_op | source)
XLA Modules:
  0.0 185.5 jit_solution(17967879734070282035)
XLA Ops:
  0.6 0.9 maximum_bitcast_fusion
  1.5 0.0 copy-start.8
  1.6 26.8 %all_to_all.56 = bf16[24,12,128]{2,1,0:T(8,128)(2,1)S(1)} all-to-all(bf16[24,12,128]{2,1,0:T(8,128)(2,1)S(1)} %copy.31), channel_id=1, replica_groups=mesh['dap'=24,'ctx'=32] {'dap'}, dimensions={0} | all-to-all | bytes 147456 | tf_op jit(solution)/shard_map/all_to_all | solution.py:239
  28.5 0.0 copy-start.2
  28.5 0.9 copy-done.2
  29.4 0.0 copy-start.6
  29.4 0.7 copy-done.6
  30.1 0.4 shard_map.131
  30.4 0.0 copy-start
  30.4 0.7 copy-done
  31.1 0.0 copy-start.4
  31.1 0.1 broadcast_in_dim.17
  31.2 28.1 %all_to_all.57 = bf16[16,144,128]{2,1,0:T(8,128)(2,1)S(1)} all-to-all(bf16[16,144,128]{2,1,0:T(8,128)(2,1)S(1)} %broadcast_in_dim.17), channel_id=1, replica_groups={{0,2,4,6,8,10,12,14,16,18,20,22,24,26,28,30},{1,3,5,7,9,11,13,15,17,19,..., dimensions={0} | all-to-all | bytes 1179648 | tf_op jit(solution)/shard_map/all_to_all | solution.py:253
  59.2 1.9 %collective-permute-start = (bf16[2304,128]{1,0:T(8,128)(2,1)S(1)}, bf16[2304,128]{1,0:T(8,128)(2,1)S(1)}, u32[]{:S(2)}, u32[]{:S(2)}) collective-permute-start(bf16[2304,128]{1,0:T(8,128)(2,1)S(1)} %bitcast.22), channel_id=1, source_target_pairs={{0,1},{1,0},{2,3},{3,2},{4,5},{5,4},{6,7},{7,6},{8,9},{9,8},{10,11... | collective-permute-start | bytes 1769480 | tf_op jit(solution)/shard_map/ppermute | solution.py:254
  61.2 0.0 copy-done.8
  61.2 0.6 broadcast_in_dim.18.mask_ref
  61.8 1.3 collective-permute-done
  63.1 0.1 broadcast_select_fusion.1
  63.2 0.0 copy-done.4
  63.3 1.1 pad_maximum_fusion.g_ref
  64.3 23.1 %shard_map.132 = (bf16[5184,128]{1,0:T(8,128)(2,1)}, bf16[4608,128]{1,0:T(8,128)(2,1)}, f32[288,128]{1,0:T(8,128)}) custom-call(bf16[4608,128]{1,0:T(8,128)(2,1)} %pad_maximum_fusion.g_ref, bf16[144,128]{1,0:T(8,128)(2,1)} %copy-done.4, f32[288,128]{1,0:T(8,128)} %copy-done, f32[288,2304]{1,0:T(8,128)} %bitcast.21, s32[1,2304]{1,0:T(1,128)} %broadcast_in_dim.18.mask_ref, ...), custom_call_target="tpu_custom_call" | custom-call | tf_op jit(solution)/shard_map/pallas_call | solution.py:258
  87.4 5.8 %all_to_all.58 = bf16[2,2304,128]{2,1,0:T(8,128)(2,1)S(1)} all-to-all(bf16[2,2304,128]{2,1,0:T(8,128)(2,1)} %bitcast.24), channel_id=1, replica_groups={{0,1},{2,3},{4,5},{6,7},{8,9},{10,11},{12,13},{14,15},{16,17},{18,19},{..., dimensions={0} | all-to-all | bytes 2359296 | tf_op jit(solution)/shard_map/all_to_all | solution.py:284
  93.2 0.0 copy-start.1
  93.2 0.0 copy-start.3
  93.2 0.0 copy-start.5
  93.2 0.0 copy-start.7
  93.2 0.6 reduce_sum.12
  93.8 24.3 %all_to_all.59.parts_ref = bf16[16,144,128]{2,1,0:T(8,128)(2,1)S(1)} all-to-all(bf16[16,144,128]{2,1,0:T(8,128)(2,1)S(1)} %bitcast.23), channel_id=1, replica_groups={{0,2,4,6,8,10,12,14,16,18,20,22,24,26,28,30},{1,3,5,7,9,11,13,15,17,19,..., dimensions={0} | all-to-all | bytes 1179648 | tf_op jit(solution)/shard_map/all_to_all | solution.py:286
  118.1 0.0 copy-done.1
  118.1 0.0 copy-done.3
  118.1 0.0 copy-done.5
  118.1 0.0 copy-done.7
  118.1 0.4 shard_map.133
  118.6 15.6 %all_to_all.60 = bf16[24,6,128]{2,1,0:T(8,128)(2,1)S(1)} all-to-all(bf16[24,6,128]{2,1,0:T(8,128)(2,1)S(1)} %all_to_all.46), channel_id=1, replica_groups=mesh['dap'=24,'ctx'=32] {'dap'}, dimensions={0} | all-to-all | bytes 73728 | tf_op jit(solution)/shard_map/all_to_all | solution.py:294
  134.2 4.9 %all-to-all-start.5 = ((bf16[24,216,128]{2,1,0:T(8,128)(2,1)}), bf16[24,216,128]{2,1,0:T(8,128)(2,1)S(1)}, u32[]{:S(2)}, u32[]{:S(2)}) async-start(bf16[24,216,128]{2,1,0:T(8,128)(2,1)} %bitcast.13), calls=%async_computation.5 | async-start | bytes 2654208 | tf_op jit(solution)/shard_map/all_to_all | solution.py:281
  139.1 0.7 copy.33
  139.8 44.7 %all-to-all-done.5.parts_ref = bf16[24,216,128]{2,1,0:T(8,128)(2,1)S(1)} async-done(((bf16[24,216,128]{2,1,0:T(8,128)(2,1)}), bf16[24,216,128]{2,1,0:T(8,128)(2,1)S(1)}, u32[]{:S(2)}, u32[]{:S(2)}) %all-to-all-start.5) | async-done | bytes 1327136 | tf_op jit(solution)/shard_map/all_to_all | solution.py:281
  184.5 1.0 shard_map.134
  (6 shorter events, 0.1 us)
Async XLA Ops:
  1.5 59.6 %copy-start.8 = (s32[2304]{0:T(1024)S(1)}, s32[2304]{0:T(1024)}, u32[]{:S(2)}) copy-start(s32[2304]{0:T(1024)} %param.14) | copy-start | bytes 27652
  28.5 0.9 copy-start.2
  29.4 0.7 copy-start.6
  30.4 0.7 copy-start
  31.1 32.2 %copy-start.4 = (bf16[144,128]{1,0:T(8,128)(2,1)}, bf16[144,128]{1,0:T(8,128)(2,1)S(1)}, u32[]{:S(2)}) copy-start(bf16[144,128]{1,0:T(8,128)(2,1)S(1)} %get-tuple-element.7.normed_ref) | copy-start | bytes 110596
  59.2 3.9 %collective-permute-start = (bf16[2304,128]{1,0:T(8,128)(2,1)S(1)}, bf16[2304,128]{1,0:T(8,128)(2,1)S(1)}, u32[]{:S(2)}, u32[]{:S(2)}) collective-permute-start(bf16[2304,128]{1,0:T(8,128)(2,1)S(1)} %bitcast.22), channel_id=1, source_target_pairs={{0,1},{1,0},{2,3},{3,2},{4,5},{5,4},{6,7},{7,6},{8,9},{9,8},{10,11... | collective-permute-start | bytes 1769480 | tf_op jit(solution)/shard_map/ppermute | solution.py:254
  93.2 24.9 %copy-start.1 = (f32[288,128]{1,0:T(8,128)S(1)}, f32[288,128]{1,0:T(8,128)}, u32[]{:S(2)}) copy-start(f32[288,128]{1,0:T(8,128)} %copy-done) | copy-start | bytes 442372
  93.2 24.9 %copy-start.3 = (f32[288,128]{1,0:T(8,128)S(1)}, f32[288,128]{1,0:T(8,128)}, u32[]{:S(2)}) copy-start(f32[288,128]{1,0:T(8,128)} %get-tuple-element.10.loc_ref) | copy-start | bytes 442372
  93.2 24.9 %copy-start.5 = (bf16[144,144]{1,0:T(8,128)(2,1)S(1)}, bf16[144,144]{1,0:T(8,128)(2,1)}, u32[]{:S(2)}) copy-start(bf16[144,144]{1,0:T(8,128)(2,1)} %constant.26.clone.order_ref) | copy-start | bytes 124420
  93.2 24.9 %copy-start.7 = (f32[128]{0:T(128)S(1)}, f32[128]{0:T(128)}, u32[]{:S(2)}) copy-start(f32[128]{0:T(128)} %param.16) | copy-start | bytes 1540
  134.2 50.3 %all-to-all-start.5 = ((bf16[24,216,128]{2,1,0:T(8,128)(2,1)}), bf16[24,216,128]{2,1,0:T(8,128)(2,1)S(1)}, u32[]{:S(2)}, u32[]{:S(2)}) async-start(bf16[24,216,128]{2,1,0:T(8,128)(2,1)} %bitcast.13), calls=%async_computation.5 | async-start | bytes 2654208 | tf_op jit(solution)/shard_map/all_to_all | solution.py:281

commit v2 on v1

v2 whole, which is shorter than its diff:
```python
import numpy as np

import jax
import jax.numpy as jnp
from jax import lax
from jax.experimental import pallas as pl
from jax.experimental.pallas import tpu as pltpu
from jax.sharding import PartitionSpec as P

C = 128
H = 4
DH = 32
SCALE = DH ** (-0.5)
F32 = jnp.float32
BF16 = jnp.bfloat16
STEP = 16
UNROLL = 3

CORES = [[2 * m, 2 * m + 1] for m in range(16)]
CHIPS = [[2 * m + r for m in range(16)] for r in range(2)]


def mm(a, b):
    return jnp.dot(a, b, preferred_element_type=F32)


def mm_t(a, b):
    return lax.dot_general(a, b, (((1,), (1,)), ((), ())), preferred_element_type=F32)


def halves(x):
    hi = x.astype(BF16)
    return hi, (x - hi.astype(F32)).astype(BF16)


def center(x):
    mean = jnp.mean(x, axis=-1, keepdims=True)
    cen = x - mean
    var = jnp.mean(cen * cen, axis=-1, keepdims=True)
    rstd = lax.rsqrt(var + 1e-05)
    return cen * rstd, rstd


def center_back(hat, rstd, gain, d_out):
    t = d_out * gain
    a = jnp.mean(t, axis=-1, keepdims=True)
    b = jnp.mean(t * hat, axis=-1, keepdims=True)
    return rstd * (t - a - hat * b)


def prep_kernel(x_ref, order_ref, gain_ref, normed_ref, both_ref):
    both = mm(order_ref[...], x_ref[...])
    both_ref[...] = both
    hat, _ = center(both[: both.shape[0] // 2])
    normed_ref[...] = (hat * gain_ref[...]).astype(BF16)


def main_kernel(
    mine_ref, other_ref, normed_ref, both_ref, bias_ref, mask_ref, w_in_ref, w_out_ref, gain_ref, w_up_ref,
    w_down_ref,
    db_ref, keep_ref, send_ref, loc_ref,
    k_scr, v_scr, s_scr, e_scr, sum_scr, ds_scr, dsb_scr, dn_scr,
):
    n = bias_ref.shape[1]
    rows = bias_ref.shape[0] // H
    cols = 2
    block = cols * rows
    pairs = n // (2 * rows)
    core = lax.rem(lax.axis_index("ctx"), 2)
    first = core == 0

    batch = 4

    def make_kv(q, _):
        at = pl.ds(pl.multiple_of(q * batch * block, batch * block), batch * block)
        mine, other = mine_ref[at, :], other_ref[at, :]
        w_kv = w_in_ref[:, C : 3 * C]
        parts = [mm(jnp.where(first, mine, other), w_kv), mm(jnp.where(first, other, mine), w_kv)]
        for t in range(batch):
            dest = pl.ds(pl.multiple_of((q * batch + t) * 2 * rows, 2 * rows), 2 * rows)
            for j in range(cols):
                base = t * block + j * rows
                kv = jnp.concatenate([part[base : base + rows] for part in parts], axis=0).astype(BF16)
                k_scr[j, dest, :] = kv[:, :C]
                v_scr[j, dest, :] = kv[:, C:]
        return 0

    lax.fori_loop(0, pairs // batch, make_kv, 0)

    normed = normed_ref[...]
    queries = mm(normed, w_in_ref[:, :C])
    gate_raw = mm(normed, w_in_ref[:, 3 * C :])
    key_bias = (mask_ref[...].astype(F32) - 1.0) * 1000000000.0

    def head_mask(h):
        lane = lax.broadcasted_iota(jnp.int32, (rows, C), 1)
        return (lane >= h * DH) & (lane < (h + 1) * DH)

    def stack(x):
        return jnp.concatenate([jnp.where(head_mask(h), x, 0.0) for h in range(H)], axis=0)

    def unstack(x):
        out = jnp.where(head_mask(0), x[:rows], 0.0)
        for h in range(1, H):
            out = jnp.where(head_mask(h), x[h * rows : (h + 1) * rows], out)
        return out

    q_stack = [stack(queries[j * rows : (j + 1) * rows]) for j in range(cols)]
    heads = []
    for j in range(cols):
        s_scr[j] = mm_t(q_stack[j].astype(BF16), k_scr[j])

        def soft(r, _, j=j):
            at = pl.ds(pl.multiple_of(r * STEP, STEP), STEP)
            s = s_scr[j, at, :] * SCALE + bias_ref[at, :] + key_bias
            e = jnp.exp(s - jnp.max(s, axis=-1, keepdims=True))
            e_scr[j, at, :] = e.astype(BF16)
            sum_scr[j, at, :] = jnp.broadcast_to(jnp.sum(e, axis=-1, keepdims=True), (STEP, C))
            return 0

        lax.fori_loop(0, H * rows // STEP, soft, 0, unroll=UNROLL)
    inv = [1.0 / sum_scr[j] for j in range(cols)]
    o_stack = [mm(e_scr[j], v_scr[j]) * inv[j] for j in range(cols)]
    heads_out = jnp.concatenate([unstack(o) for o in o_stack], axis=0)

    open_ = jax.nn.sigmoid(gate_raw)
    source, cot = both_ref[:block, :], both_ref[block:, :]
    gated = (heads_out * open_).astype(BF16)
    mid = source + mm(gated, w_out_ref[...])
    mid_hat, mid_rstd = center(mid)
    gain = gain_ref[...]
    pre = mm((mid_hat * gain).astype(BF16), w_up_ref[...])
    gs = jax.nn.sigmoid(pre)
    slope = gs + pre * gs * (1.0 - gs)
    d_hidden = (mm_t(cot.astype(BF16), w_down_ref[...]) * slope).astype(BF16)
    d_trans = mm_t(d_hidden, w_up_ref[...])
    d_mid = cot + center_back(mid_hat, mid_rstd, gain, d_trans)
    d_gated = mm_t(d_mid.astype(BF16), w_out_ref[...])
    d_heads = d_gated * open_
    d_gate = d_gated * heads_out * open_ * (1.0 - open_)
    loc_ref[:block, :] = d_mid

    w_kv = w_in_ref[:, C : 3 * C]
    d_query = []
    for j in range(cols):
        do_f = stack(d_heads[j * rows : (j + 1) * rows]).astype(BF16).astype(F32) * inv[j]
        do_stack = do_f.astype(BF16)
        dot_row = jnp.sum(o_stack[j] * do_stack.astype(F32), axis=-1, keepdims=True)
        sum_scr[j] = jnp.broadcast_to(dot_row, (H * rows, C))
        s_scr[j] = mm_t(do_stack, v_scr[j])

        def back(r, _, j=j):
            at = pl.ds(pl.multiple_of(r * STEP, STEP), STEP)
            ds = e_scr[j, at, :].astype(F32) * (s_scr[j, at, :] - sum_scr[j, at, :1])
            dsb_scr[j, at, :] = ds.astype(BF16)
            if j == 0:
                ds_scr[at, :] = ds
            else:
                ds_scr[at, :] = ds_scr[at, :] + ds
            return 0

        lax.fori_loop(0, H * rows // STEP, back, 0, unroll=UNROLL)
        ds_b = dsb_scr[j]
        d_query.append(unstack(mm(ds_b, k_scr[j])) * SCALE)
        dk = mm(q_stack[j].T.astype(BF16), ds_b) * SCALE
        dv = mm(do_f.T.astype(BF16), e_scr[j])
        dn_scr[j] = mm(w_kv, jnp.concatenate([dk, dv], axis=0).astype(BF16)).T

    hi, lo = halves(jnp.concatenate([jnp.concatenate(d_query, axis=0), d_gate], axis=1))
    w_qg = jnp.concatenate([w_in_ref[:, :C], w_in_ref[:, 3 * C :]], axis=1)
    loc_ref[block:, :] = mm_t(hi, w_qg) + mm_t(lo, w_qg)

    for p in range(pairs):
        place = sum(((p >> bit) & 1) << to for bit, to in ((0, 0), (3, 1), (2, 2), (1, 3))) * block
        for ref, which in ((keep_ref, core), (send_ref, 1 - core)):
            at = pl.ds(pl.multiple_of((2 * p + which) * rows, rows), rows)
            both = jnp.concatenate([dn_scr[j, at, :] for j in range(cols)], axis=0)
            ref[place : place + block, :] = both.astype(ref.dtype)

    def put_db(t, _):
        at = pl.ds(pl.multiple_of(t * C, C), C)
        xs = [ds_scr[pl.ds(h * rows, rows), at] for h in range(H)]
        groups = []
        for a in range(4):
            out = xs[a]
            for h in range(H):
                if h != a:
                    out = jnp.where(head_mask(h), pltpu.roll(xs[h], ((h - a) * DH) % C, 1), out)
            groups.append(out)
        start = pl.multiple_of(t * 4 * rows, 4 * rows)
        db_ref[pl.ds(start, 4 * rows), :] = jnp.concatenate(groups, axis=0).astype(BF16)
        return 0

    lax.fori_loop(0, n // C, put_db, 0)


def last_kernel(parts_ref, loc_ref, both_ref, gain_ref, order_ref, after_ref, out_ref):
    del after_ref
    half = loc_ref.shape[0] // 2
    total = loc_ref[half:, :] + parts_ref[...]
    hat, rstd = center(both_ref[:half, :])
    d_pair = loc_ref[:half, :] + center_back(hat, rstd, gain_ref[...], total)
    out_ref[...] = mm(order_ref[...], d_pair.astype(BF16)).astype(BF16)


def bias_kernel(parts_ref, out_ref):
    rows = out_ref.shape[1]
    total = parts_ref[0].astype(F32)
    for p in range(1, parts_ref.shape[0]):
        total = total + parts_ref[p].astype(F32)
    for h in range(H):
        out_ref[h] = jnp.concatenate(
            [total[t * rows : (t + 1) * rows, h * DH : (h + 1) * DH] for t in range(3)], axis=1
        )


def call(kernel, out_shape, scratch=(), limit=48, n_in=None, unread=0):
    specs = {}
    if unread:
        vmem = pl.BlockSpec(memory_space=pltpu.VMEM)
        specs["in_specs"] = [vmem] * (n_in - unread) + [pl.BlockSpec(memory_space=pl.ANY)] * unread
    return pl.pallas_call(
        kernel,
        out_shape=out_shape,
        **specs,
        scratch_shapes=list(scratch),
        compiler_params=pltpu.CompilerParams(vmem_limit_bytes=limit * 1024 * 1024),
    )


def one_hot(source_of):
    out = np.zeros((len(source_of), len(source_of)), np.float32)
    out[np.arange(len(source_of)), source_of] = 1.0
    return out


def per_device(pair, cotangent, residue_mask, bias, ln_attend, w_in, w_out, ln_trans, w_up, w_down):
    n_dap = lax.axis_size("dap")
    n_ctx = lax.axis_size("ctx")
    local, n_cols, _ = pair.shape
    cols = n_cols // n_dap
    rows = local * n_dap
    n = rows * n_ctx
    block = cols * rows
    each = cols * local

    both = jnp.stack([pair, cotangent]).reshape(2, local, n_dap, cols, C)
    both = both.transpose(2, 0, 3, 1, 4).reshape(n_dap * 2 * each, C)
    both = lax.all_to_all(both, "dap", 0, 0, tiled=True)
    source_of = [
        (i // local) * 2 * each + a * each + j * local + i % local
        for a in range(2)
        for j in range(cols)
        for i in range(rows)
    ]
    normed, both = call(
        prep_kernel,
        (jax.ShapeDtypeStruct((block, C), BF16), jax.ShapeDtypeStruct((2 * block, C), F32)),
    )(both, jnp.asarray(one_hot(source_of), BF16), ln_attend[None])

    gathered = jnp.broadcast_to(normed[None], (n_ctx // 2, block, C)).reshape(n_ctx // 2 * block, C)
    gathered = lax.all_to_all(gathered, "ctx", 0, 0, tiled=True, axis_index_groups=CHIPS)
    other = lax.ppermute(gathered, "ctx", [(i, i ^ 1) for i in range(n_ctx)])

    half = jax.ShapeDtypeStruct((n * cols // 2, C), F32)
    db, keep, send, loc = call(
        main_kernel,
        (
            jax.ShapeDtypeStruct((n // DH * rows, C), BF16),
            half,
            jax.ShapeDtypeStruct(half.shape, BF16),
            jax.ShapeDtypeStruct((2 * block, C), F32),
        ),
        scratch=(
            pltpu.VMEM((cols, n, C), BF16),
            pltpu.VMEM((cols, n, C), BF16),
            pltpu.VMEM((cols, H * rows, n), F32),
            pltpu.VMEM((cols, H * rows, n), BF16),
            pltpu.VMEM((cols, H * rows, C), F32),
            pltpu.VMEM((H * rows, n), F32),
            pltpu.VMEM((cols, H * rows, n), BF16),
            pltpu.VMEM((cols, n, C), F32),
        ),
        limit=40,
    )(
        gathered, other, normed, both, bias.reshape(H * rows, n), residue_mask[None], w_in, w_out, ln_trans[None],
        w_up, w_down,
    )

    db = lax.all_to_all(db, "dap", 0, 0, tiled=True).reshape(n_dap, n // n_dap // DH * rows, C)

    here = lax.axis_index("ctx")
    total = keep + lax.ppermute(send, "ctx", [(i, i ^ 1) for i in range(n_ctx)]).astype(F32)
    for flip in (4, 8, 16, 2):
        total = total.reshape(2, -1, C)
        bit = jnp.where((here & flip) != 0, 1, 0)
        kept = lax.dynamic_index_in_dim(total, bit, 0, False)
        sent = lax.dynamic_index_in_dim(total, 1 - bit, 0, False).astype(BF16)
        total = kept + lax.ppermute(sent, "ctx", [(i, i ^ flip) for i in range(n_ctx)]).astype(F32)

    back_of = [
        j * rows + d * local + r for d in range(n_dap) for r in range(local) for j in range(cols)
    ]
    d_pair = call(last_kernel, jax.ShapeDtypeStruct((block, C), BF16), n_in=6, unread=1)(
        total, loc, both, ln_attend[None], jnp.asarray(one_hot(back_of), BF16), db
    )
    bias_grad = call(bias_kernel, jax.ShapeDtypeStruct((H, rows, n // n_dap), F32))(db)
    d_pair = lax.all_to_all(d_pair, "dap", 0, 0, tiled=True).reshape(n_dap, local, cols, C)
    pair_grad = d_pair.transpose(1, 0, 2, 3).reshape(local, n_cols, C).astype(F32)
    return (pair_grad, bias_grad)


def solution(mesh):
    in_specs = (
        P(("ctx", "dap"), None, None),
        P(("ctx", "dap"), None, None),
        P(),
        P(None, "ctx", None),
        P(),
        P(),
        P(),
        P(),
        P(),
        P(),
    )
    out_specs = (P(("ctx", "dap"), None, None), P(None, "ctx", "dap"))
    return jax.shard_map(
        per_device, mesh=mesh, in_specs=in_specs, out_specs=out_specs, check_vma=False
    )
```

time: 186 us -> 159 us (0.85)
  blocking collectives: 101 us -> 55.2 us
  starting transfers between devices: 6.77 us -> 30 us
  Pallas kernels: 24.8 us -> 16.4 us
  local copies, waits for them, and re-layouts: 3.71 us -> 8.77 us
  waiting for transfers between devices: 46.1 us -> 42 us
    all_to_all x3 -> x0, blocking collectives: 45.7 us -> none  [the longest x1 24.3 us: per_device(): lax.all_to_all(dn, 'ctx', 0, 0, tiled=True, axis_index_groups=CHIPS)]
    all_to_all x1, waiting for transfers between devices: 44.7 us -> 0.01 us  [per_device(): lax.all_to_all(db, 'dap', 0, 0, tiled=True)]
    ppermute x0 -> x5, waiting for transfers between devices: none -> 31.9 us  [the longest x4 29.8 us: per_device(): lax.ppermute(sent, 'ctx', [(i, i ^ flip) for i in range(n_ctx)]).astype(F32)]
    ppermute x0 -> x5, starting transfers between devices: none -> 11.5 us  [the longest x4 9.59 us: per_device(): lax.ppermute(sent, 'ctx', [(i, i ^ flip) for i in range(n_ctx)]).astype(F32)]
    all_to_all x0 -> x1, starting transfers between devices: none -> 10.6 us  [per_device(): lax.all_to_all(d_pair, 'dap', 0, 0, tiled=True)]
    all_to_all x0 -> x1, waiting for transfers between devices: none -> 8.93 us  [per_device(): lax.all_to_all(d_pair, 'dap', 0, 0, tiled=True)]
    pallas_call x2, Pallas kernels: 23.5 us -> 15.1 us  [the longest x1 14.7 us: per_device(): call(main_kernel, (jax.ShapeDtypeStruct((n // DH * rows, C), BF16), half,...]
    add x0 -> x5, other arithmetic: none -> 3.37 us  [the longest x1 2.19 us: per_device(): keep + lax.ppermute(send, 'ctx', [(i, i ^ 1) for i in range(n_ctx)]).asty...]
  transfers between devices with their start and end apart: 2 -> 8, of which waited for: 2 -> 7; matrix products, arithmetic and copies ran while one was open for 1% -> 3% of each run, Pallas kernels for 0% -> 1%
where the time goes in v2:
time: 159 us; the launch traced here: 158 us
  blocking collectives  55.2 us (35%)
  waiting for transfers between devices  42 us (26%)
  starting transfers between devices  30 us (19%)
  Pallas kernels  16.4 us (10%)
  local copies, waits for them, and re-layouts  8.77 us (6%)
  other arithmetic  4.31 us (3%)
    ppermute x4, waiting for transfers between devices, per_device(): lax.ppermute(sent, 'ctx', [(i, i ^ flip) for i in range(n_ctx)]).astype(F32)  29.8 us
    all_to_all x1, blocking collectives, per_device(): lax.all_to_all(gathered, 'ctx', 0, 0, tiled=True, axis_index_groups=CHIPS)  28.1 us
    all_to_all x1, blocking collectives, per_device(): both = lax.all_to_all(both, 'dap', 0, 0, tiled=True)  27.1 us
    pallas_call x1, Pallas kernels, per_device(): call(main_kernel, (jax.ShapeDtypeStruct((n // DH * rows, C), BF16), half,...  14.7 us
    all_to_all x1, starting transfers between devices, per_device(): lax.all_to_all(d_pair, 'dap', 0, 0, tiled=True)  10.6 us
    ppermute x4, starting transfers between devices, per_device(): lax.ppermute(sent, 'ctx', [(i, i ^ flip) for i in range(n_ctx)]).astype(F32)  9.59 us
    all_to_all x1, waiting for transfers between devices, per_device(): lax.all_to_all(d_pair, 'dap', 0, 0, tiled=True)  8.93 us
    all_to_all x1, starting transfers between devices, per_device(): lax.all_to_all(db, 'dap', 0, 0, tiled=True)  6.04 us
  transfers between devices with their start and end apart: 8, of which 7 were waited for; matrix products, arithmetic and copies ran while one was open for 3% of the time, Pallas kernels for 1%

profile of v2, /device:TPU:2, one launch (start us, length us, event | category | flops | bytes accessed | tf_op | source)
XLA Modules:
  0.0 157.8 jit_solution(11428330330831163282)
XLA Ops:
  0.6 0.0 copy-start.6
  0.6 0.0 copy-start.9
  0.7 0.9 maximum_bitcast_fusion
  1.6 0.0 copy-start.5
  1.6 0.0 copy-start
  1.7 27.1 %all_to_all.37 = bf16[24,12,128]{2,1,0:T(8,128)(2,1)S(1)} all-to-all(bf16[24,12,128]{2,1,0:T(8,128)(2,1)S(1)} %copy.31), channel_id=1, replica_groups=mesh['dap'=24,'ctx'=32] {'dap'}, dimensions={0} | all-to-all | bytes 147456 | tf_op jit(solution)/shard_map/all_to_all | solution.py:249
  28.8 0.0 copy-start.4
  28.8 0.9 copy-done.4
  29.7 0.7 copy-done.10
  30.4 0.4 shard_map.131
  30.7 0.1 broadcast_in_dim.17
  30.8 28.1 %all_to_all.38 = bf16[16,144,128]{2,1,0:T(8,128)(2,1)S(1)} all-to-all(bf16[16,144,128]{2,1,0:T(8,128)(2,1)S(1)} %broadcast_in_dim.17), channel_id=1, replica_groups={{0,2,4,6,8,10,12,14,16,18,20,22,24,26,28,30},{1,3,5,7,9,11,13,15,17,19,..., dimensions={0} | all-to-all | bytes 1179648 | tf_op jit(solution)/shard_map/all_to_all | solution.py:262
  58.9 1.9 %collective-permute-start = (bf16[2304,128]{1,0:T(8,128)(2,1)S(1)}, bf16[2304,128]{1,0:T(8,128)(2,1)S(1)}, u32[]{:S(2)}, u32[]{:S(2)}) collective-permute-start(bf16[2304,128]{1,0:T(8,128)(2,1)S(1)} %bitcast.36), channel_id=1, source_target_pairs={{0,1},{1,0},{2,3},{3,2},{4,5},{5,4},{6,7},{7,6},{8,9},{9,8},{10,11... | collective-permute-start | bytes 1769480 | tf_op jit(solution)/shard_map/ppermute | solution.py:263
  60.8 0.7 broadcast_in_dim.18.mask_ref
  61.5 1.3 collective-permute-done.other_ref
  62.8 0.0 copy-done.6
  62.8 0.0 copy-done
  62.8 0.0 copy-done.12
  62.8 0.0 copy-start.7
  62.8 0.9 copy-done.7
  63.7 14.7 %shard_map.132 = (bf16[5184,128]{1,0:T(8,128)(2,1)S(1)}, f32[2304,128]{1,0:T(8,128)S(1)}, bf16[2304,128]{1,0:T(8,128)(2,1)S(1)}, f32[288,128]{1,0:T(8,128)S(1)}) custom-call(bf16[2304,128]{1,0:T(8,128)(2,1)S(1)} %bitcast.37, bf16[2304,128]{1,0:T(8,128)(2,1)S(1)} %collective-permute-done.other_ref, bf16[144,128]{1,0:T(8,128)(2,1)S(1)} %get-tuple-element.8.normed_ref, ...), custom_call_target="tpu_custom_call" | custom-call | tf_op jit(solution)/shard_map/pallas_call | solution.py:266
  78.5 1.0 copy-done.2
  79.5 0.8 copy-done.13
  80.3 1.1 copy-done.1
  81.4 6.0 %all-to-all-start.2 = ((bf16[24,216,128]{2,1,0:T(8,128)(2,1)}), bf16[24,216,128]{2,1,0:T(8,128)(2,1)S(1)}, u32[]{:S(2)}, u32[]{:S(2)}) async-start(bf16[24,216,128]{2,1,0:T(8,128)(2,1)} %bitcast.38), calls=%async_computation.2 | async-start | bytes 2654208 | tf_op jit(solution)/shard_map/all_to_all | solution.py:290
  87.4 0.0 copy-done.14
  87.4 1.9 %collective-permute-start.1 = (bf16[2304,128]{1,0:T(8,128)(2,1)S(1)}, bf16[2304,128]{1,0:T(8,128)(2,1)}, u32[]{:S(2)}, u32[]{:S(2)}) collective-permute-start(bf16[2304,128]{1,0:T(8,128)(2,1)S(1)} %copy-done.14), channel_id=1, source_target_pairs={{0,1},{1,0},{2,3},{3,2},{4,5},{5,4},{6,7},{7,6},{8,9},{9,8},{10,11... | collective-permute-start | bytes 1769480 | tf_op jit(solution)/shard_map/ppermute | solution.py:293
  89.4 2.1 %collective-permute-done.1 = bf16[2304,128]{1,0:T(8,128)(2,1)} collective-permute-done((bf16[2304,128]{1,0:T(8,128)(2,1)S(1)}, bf16[2304,128]{1,0:T(8,128)(2,1)}, u32[]{:S(2)}, u32[]{:S(2)}) %collective-permute-start.1) | collective-permute-done | bytes 589856 | tf_op jit(solution)/shard_map/ppermute | solution.py:293
  91.5 2.2 %convert_add_fusion = f32[2304,128]{1,0:T(8,128)} fusion(f32[2304,128]{1,0:T(8,128)S(1)} %copy-done.3, bf16[2304,128]{1,0:T(8,128)(2,1)} %collective-permute-done.1), kind=kLoop, calls=%fused_computation | loop fusion | flops 589824 | bytes 2949120 | tf_op jit(solution)/shard_map/add | solution.py:293
  93.7 1.1 fusion
  94.8 2.4 %collective-permute-start.2 = (bf16[1152,128]{1,0:T(8,128)(2,1)S(1)}, bf16[1152,128]{1,0:T(8,128)(2,1)S(1)}, u32[]{:S(2)}, u32[]{:S(2)}) collective-permute-start(bf16[1152,128]{1,0:T(8,128)(2,1)S(1)} %fusion), channel_id=1, source_target_pairs={{0,4},{1,5},{2,6},{3,7},{4,0},{5,1},{6,2},{7,3},{8,12},{9,13},{10,... | collective-permute-start | bytes 884744 | tf_op jit(solution)/shard_map/ppermute | solution.py:299
  97.2 8.5 %collective-permute-done.2 = bf16[1152,128]{1,0:T(8,128)(2,1)S(1)} collective-permute-done((bf16[1152,128]{1,0:T(8,128)(2,1)S(1)}, bf16[1152,128]{1,0:T(8,128)(2,1)S(1)}, u32[]{:S(2)}, u32[]{:S(2)}) %collective-permute-start.2) | collective-permute-done | bytes 294944 | tf_op jit(solution)/shard_map/ppermute | solution.py:299
  105.7 1.1 bitcast_add_fusion
  106.8 0.0 copy-start.8
  106.8 0.0 copy-start.11
  106.9 2.5 %collective-permute-start.3 = (bf16[576,128]{1,0:T(8,128)(2,1)S(1)}, bf16[576,128]{1,0:T(8,128)(2,1)S(1)}, u32[]{:S(2)}, u32[]{:S(2)}) collective-permute-start(bf16[576,128]{1,0:T(8,128)(2,1)S(1)} %fusion.1), channel_id=1, source_target_pairs={{0,8},{1,9},{2,10},{3,11},{4,12},{5,13},{6,14},{7,15},{8,0},{9,1},... | collective-permute-start | bytes 442376 | tf_op jit(solution)/shard_map/ppermute | solution.py:299
  109.4 8.4 %collective-permute-done.3 = bf16[576,128]{1,0:T(8,128)(2,1)S(1)} collective-permute-done((bf16[576,128]{1,0:T(8,128)(2,1)S(1)}, bf16[576,128]{1,0:T(8,128)(2,1)S(1)}, u32[]{:S(2)}, u32[]{:S(2)}) %collective-permute-start.3) | collective-permute-done | bytes 147488 | tf_op jit(solution)/shard_map/ppermute | solution.py:299
  117.9 2.7 %collective-permute-start.4 = (bf16[288,128]{1,0:T(8,128)(2,1)S(1)}, bf16[288,128]{1,0:T(8,128)(2,1)S(1)}, u32[]{:S(2)}, u32[]{:S(2)}) collective-permute-start(bf16[288,128]{1,0:T(8,128)(2,1)S(1)} %fusion.2), channel_id=1, source_target_pairs={{0,16},{1,17},{2,18},{3,19},{4,20},{5,21},{6,22},{7,23},{8,24},{9,... | collective-permute-start | bytes 221192 | tf_op jit(solution)/shard_map/ppermute | solution.py:299
  120.6 7.5 %collective-permute-done.4 = bf16[288,128]{1,0:T(8,128)(2,1)S(1)} collective-permute-done((bf16[288,128]{1,0:T(8,128)(2,1)S(1)}, bf16[288,128]{1,0:T(8,128)(2,1)S(1)}, u32[]{:S(2)}, u32[]{:S(2)}) %collective-permute-start.4) | collective-permute-done | bytes 73760 | tf_op jit(solution)/shard_map/ppermute | solution.py:299
  128.1 2.0 %collective-permute-start.5 = (bf16[144,128]{1,0:T(8,128)(2,1)S(1)}, bf16[144,128]{1,0:T(8,128)(2,1)S(1)}, u32[]{:S(2)}, u32[]{:S(2)}) collective-permute-start(bf16[144,128]{1,0:T(8,128)(2,1)S(1)} %fusion.3), channel_id=1, source_target_pairs={{0,2},{1,3},{2,0},{3,1},{4,6},{5,7},{6,4},{7,5},{8,10},{9,11},{10,... | collective-permute-start | bytes 110600 | tf_op jit(solution)/shard_map/ppermute | solution.py:299
  130.1 5.4 %collective-permute-done.5 = bf16[144,128]{1,0:T(8,128)(2,1)S(1)} collective-permute-done((bf16[144,128]{1,0:T(8,128)(2,1)S(1)}, bf16[144,128]{1,0:T(8,128)(2,1)S(1)}, u32[]{:S(2)}, u32[]{:S(2)}) %collective-permute-start.5) | collective-permute-done | bytes 36896 | tf_op jit(solution)/shard_map/ppermute | solution.py:299
  135.5 0.0 all-to-all-done.2.after_ref.parts_ref
  135.5 0.4 shard_map.133
  135.9 0.6 all_to_all.31
  136.6 10.6 %all-to-all-start.3 = ((bf16[24,6,128]{2,1,0:T(8,128)(2,1)}), bf16[24,6,128]{2,1,0:T(8,128)(2,1)S(1)}, u32[]{:S(2)}, u32[]{:S(2)}) async-start(bf16[24,6,128]{2,1,0:T(8,128)(2,1)} %all_to_all.31), calls=%async_computation.3 | async-start | bytes 98304 | tf_op jit(solution)/shard_map/all_to_all | solution.py:308
  147.2 1.0 shard_map.134
  148.1 8.9 %all-to-all-done.3 = bf16[24,6,128]{2,1,0:T(8,128)(2,1)S(1)} async-done(((bf16[24,6,128]{2,1,0:T(8,128)(2,1)}), bf16[24,6,128]{2,1,0:T(8,128)(2,1)S(1)}, u32[]{:S(2)}, u32[]{:S(2)}) %all-to-all-start.3) | async-done | bytes 36896 | tf_op jit(solution)/shard_map/all_to_all | solution.py:308
  157.1 0.7 copy.33
  (23 shorter events, 0.2 us)
Async XLA Ops:
  0.6 62.2 %copy-start.6 = (bf16[128,512]{1,0:T(8,128)(2,1)S(1)}, bf16[128,512]{1,0:T(8,128)(2,1)}, u32[]{:S(2)}) copy-start(bf16[128,512]{1,0:T(8,128)(2,1)} %w_up_ref.1) | copy-start | bytes 393220
  0.6 62.2 %copy-start.9 = (bf16[128,128]{1,0:T(8,128)(2,1)S(1)}, bf16[128,128]{1,0:T(8,128)(2,1)}, u32[]{:S(2)}) copy-start(bf16[128,128]{1,0:T(8,128)(2,1)} %w_out_ref.1) | copy-start | bytes 98308
  1.6 61.2 %copy-start.5 = (bf16[128,512]{1,0:T(8,128)(2,1)S(1)}, bf16[128,512]{1,0:T(8,128)(2,1)}, u32[]{:S(2)}) copy-start(bf16[128,512]{1,0:T(8,128)(2,1)} %w_in_ref.1) | copy-start | bytes 393220
  1.6 61.2 %copy-start = (f32[4,72,2304]{2,1,0:T(8,128)S(1)}, f32[4,72,2304]{2,1,0:T(8,128)}, u32[]{:S(2)}) copy-start(f32[4,72,2304]{2,1,0:T(8,128)} %param.15) | copy-start | bytes 7962628
  28.8 0.9 copy-start.4
  29.7 0.7 copy-start.10
  30.4 32.4 %copy-start.12 = (f32[128]{0:T(128)S(1)}, f32[128]{0:T(128)}, u32[]{:S(2)}) copy-start(f32[128]{0:T(128)} %param.19) | copy-start | bytes 1540
  58.9 3.9 %collective-permute-start = (bf16[2304,128]{1,0:T(8,128)(2,1)S(1)}, bf16[2304,128]{1,0:T(8,128)(2,1)S(1)}, u32[]{:S(2)}, u32[]{:S(2)}) collective-permute-start(bf16[2304,128]{1,0:T(8,128)(2,1)S(1)} %bitcast.36), channel_id=1, source_target_pairs={{0,1},{1,0},{2,3},{3,2},{4,5},{5,4},{6,7},{7,6},{8,9},{9,8},{10,11... | collective-permute-start | bytes 1769480 | tf_op jit(solution)/shard_map/ppermute | solution.py:263
  62.8 0.9 copy-start.7
  78.5 1.0 copy-start.2
  79.5 0.8 copy-start.13
  80.3 1.1 copy-start.1
  81.4 6.1 %copy-start.14 = (bf16[2304,128]{1,0:T(8,128)(2,1)S(1)}, bf16[2304,128]{1,0:T(8,128)(2,1)}, u32[]{:S(2)}) copy-start(bf16[2304,128]{1,0:T(8,128)(2,1)} %copy-done.13) | copy-start | bytes 1769476
  81.4 10.1 %copy-start.3 = (f32[2304,128]{1,0:T(8,128)S(1)}, f32[2304,128]{1,0:T(8,128)}, u32[]{:S(2)}) copy-start(f32[2304,128]{1,0:T(8,128)} %copy-done.2) | copy-start | bytes 3538948
  81.4 54.1 %all-to-all-start.2 = ((bf16[24,216,128]{2,1,0:T(8,128)(2,1)}), bf16[24,216,128]{2,1,0:T(8,128)(2,1)S(1)}, u32[]{:S(2)}, u32[]{:S(2)}) async-start(bf16[24,216,128]{2,1,0:T(8,128)(2,1)} %bitcast.38), calls=%async_computation.2 | async-start | bytes 2654208 | tf_op jit(solution)/shard_map/all_to_all | solution.py:290
  87.4 4.0 %collective-permute-start.1 = (bf16[2304,128]{1,0:T(8,128)(2,1)S(1)}, bf16[2304,128]{1,0:T(8,128)(2,1)}, u32[]{:S(2)}, u32[]{:S(2)}) collective-permute-start(bf16[2304,128]{1,0:T(8,128)(2,1)S(1)} %copy-done.14), channel_id=1, source_target_pairs={{0,1},{1,0},{2,3},{3,2},{4,5},{5,4},{6,7},{7,6},{8,9},{9,8},{10,11... | collective-permute-start | bytes 1769480 | tf_op jit(solution)/shard_map/ppermute | solution.py:293
  94.8 10.9 %collective-permute-start.2 = (bf16[1152,128]{1,0:T(8,128)(2,1)S(1)}, bf16[1152,128]{1,0:T(8,128)(2,1)S(1)}, u32[]{:S(2)}, u32[]{:S(2)}) collective-permute-start(bf16[1152,128]{1,0:T(8,128)(2,1)S(1)} %fusion), channel_id=1, source_target_pairs={{0,4},{1,5},{2,6},{3,7},{4,0},{5,1},{6,2},{7,3},{8,12},{9,13},{10,... | collective-permute-start | bytes 884744 | tf_op jit(solution)/shard_map/ppermute | solution.py:299
  106.8 28.7 %copy-start.8 = (bf16[144,144]{1,0:T(8,128)(2,1)S(1)}, bf16[144,144]{1,0:T(8,128)(2,1)}, u32[]{:S(2)}) copy-start(bf16[144,144]{1,0:T(8,128)(2,1)} %constant.54.clone.order_ref) | copy-start | bytes 124420
  106.8 28.7 %copy-start.11 = (f32[128]{0:T(128)S(1)}, f32[128]{0:T(128)}, u32[]{:S(2)}) copy-start(f32[128]{0:T(128)} %param.16) | copy-start | bytes 1540
  106.9 11.0 %collective-permute-start.3 = (bf16[576,128]{1,0:T(8,128)(2,1)S(1)}, bf16[576,128]{1,0:T(8,128)(2,1)S(1)}, u32[]{:S(2)}, u32[]{:S(2)}) collective-permute-start(bf16[576,128]{1,0:T(8,128)(2,1)S(1)} %fusion.1), channel_id=1, source_target_pairs={{0,8},{1,9},{2,10},{3,11},{4,12},{5,13},{6,14},{7,15},{8,0},{9,1},... | collective-permute-start | bytes 442376 | tf_op jit(solution)/shard_map/ppermute | solution.py:299
  117.9 10.2 %collective-permute-start.4 = (bf16[288,128]{1,0:T(8,128)(2,1)S(1)}, bf16[288,128]{1,0:T(8,128)(2,1)S(1)}, u32[]{:S(2)}, u32[]{:S(2)}) collective-permute-start(bf16[288,128]{1,0:T(8,128)(2,1)S(1)} %fusion.2), channel_id=1, source_target_pairs={{0,16},{1,17},{2,18},{3,19},{4,20},{5,21},{6,22},{7,23},{8,24},{9,... | collective-permute-start | bytes 221192 | tf_op jit(solution)/shard_map/ppermute | solution.py:299
  128.1 7.4 %collective-permute-start.5 = (bf16[144,128]{1,0:T(8,128)(2,1)S(1)}, bf16[144,128]{1,0:T(8,128)(2,1)S(1)}, u32[]{:S(2)}, u32[]{:S(2)}) collective-permute-start(bf16[144,128]{1,0:T(8,128)(2,1)S(1)} %fusion.3), channel_id=1, source_target_pairs={{0,2},{1,3},{2,0},{3,1},{4,6},{5,7},{6,4},{7,5},{8,10},{9,11},{10,... | collective-permute-start | bytes 110600 | tf_op jit(solution)/shard_map/ppermute | solution.py:299
  136.6 20.5 %all-to-all-start.3 = ((bf16[24,6,128]{2,1,0:T(8,128)(2,1)}), bf16[24,6,128]{2,1,0:T(8,128)(2,1)S(1)}, u32[]{:S(2)}, u32[]{:S(2)}) async-start(bf16[24,6,128]{2,1,0:T(8,128)(2,1)} %all_to_all.31), calls=%async_computation.3 | async-start | bytes 98304 | tf_op jit(solution)/shard_map/all_to_all | solution.py:308

commit v3 on v2

v3 whole, which is shorter than its diff:
```python
import jax
import jax.numpy as jnp
from jax import lax
from jax.experimental import pallas as pl
from jax.experimental.pallas import tpu as pltpu
from jax.sharding import PartitionSpec as P

C = 128
H = 4
DH = 32
SCALE = DH ** (-0.5)
F32 = jnp.float32
BF16 = jnp.bfloat16
STEP = 16
UNROLL = 18
UDB = 6
LIMIT = 40
FLIPS = ((4, 8, 12), (2, 16, 18))

CORES = [[2 * m, 2 * m + 1] for m in range(16)]
CHIPS = [[2 * m + r for m in range(16)] for r in range(2)]


def mm(a, b):
    return jnp.dot(a, b, preferred_element_type=F32)


def mm_t(a, b):
    return lax.dot_general(a, b, (((1,), (1,)), ((), ())), preferred_element_type=F32)


def halves(x):
    hi = x.astype(BF16)
    return hi, (x - hi.astype(F32)).astype(BF16)


def center(x):
    mean = jnp.mean(x, axis=-1, keepdims=True)
    cen = x - mean
    var = jnp.mean(cen * cen, axis=-1, keepdims=True)
    rstd = lax.rsqrt(var + 1e-05)
    return cen * rstd, rstd


def center_back(hat, rstd, gain, d_out):
    t = d_out * gain
    a = jnp.mean(t, axis=-1, keepdims=True)
    b = jnp.mean(t * hat, axis=-1, keepdims=True)
    return rstd * (t - a - hat * b)


def iotas(rows, cols):
    shape = (rows, cols)
    return lax.broadcasted_iota(jnp.int32, shape, 0), lax.broadcasted_iota(jnp.int32, shape, 1)


def split8(at, local):
    q = at & 7
    j = jnp.where(q >= local, 1, 0)
    return j, q - local * j, q < 2 * local


def pick(where):
    return jnp.where(where, 1.0, 0.0).astype(BF16)


def first_kernel(pair_ref, cot_ref, out_ref):
    local, n_cols, _ = pair_ref.shape
    each = local * n_cols
    tokens = jnp.concatenate([pair_ref[...].reshape(each, C), cot_ref[...].reshape(each, C)], axis=0)
    out, at = iotas(out_ref.shape[0], 2 * each)
    j, r, valid = split8(out, local)
    source = ((out >> 3) & 1) * each + r * n_cols + (out >> 4) * 2 + j
    out_ref[...] = mm(pick(valid & (at == source)), tokens).astype(BF16)


def prep_kernel(x_ref, gain_ref, normed_ref, both_ref):
    block = normed_ref.shape[0]
    local = block // 2 // (x_ref.shape[0] // 16)
    out, at = iotas(2 * block, x_ref.shape[0])
    j, r, valid = split8(at, local)
    goal = ((at >> 3) & 1) * block + j * (block // 2) + (at >> 4) * local + r
    both = mm(pick(valid & (out == goal)), x_ref[...])
    both_ref[...] = both
    hat, _ = center(both[:block])
    normed_ref[...] = (hat * gain_ref[...]).astype(BF16)


def relative(place):
    return (place >> 2 << 1) | ((place >> 1 & 1) << 3) | (place & 1)


def main_kernel(
    mine_ref, other_ref, normed_ref, both_ref, bias_ref, mask_ref, w_in_ref, w_out_ref, gain_ref, w_up_ref,
    w_down_ref,
    db_out, keep_out, send_out, loc_out,
    db_ref, keep_ref, send_ref, loc_ref, sems,
    k_scr, v_scr, s_scr, e_scr, sum_scr, ds_scr, dsb_scr, dn_scr,
):
    n = bias_ref.shape[1]
    rows = bias_ref.shape[0] // H
    cols = 2
    block = cols * rows
    pairs = n // (2 * rows)
    core = lax.rem(lax.axis_index("ctx"), 2)
    first = core == 0

    outs = ((db_ref, db_out), (keep_ref, keep_out), (send_ref, send_out), (loc_ref, loc_out))
    copies = [pltpu.make_async_copy(src, dst, sems.at[i]) for i, (src, dst) in enumerate(outs)]
    batch = 4

    def make_kv(q, _):
        at = pl.ds(pl.multiple_of(q * batch * block, batch * block), batch * block)
        mine, other = mine_ref[at, :], other_ref[at, :]
        w_kv = w_in_ref[:, C : 3 * C]
        parts = [mm(jnp.where(first, mine, other), w_kv), mm(jnp.where(first, other, mine), w_kv)]
        for t in range(batch):
            dest = pl.ds(pl.multiple_of((q * batch + t) * 2 * rows, 2 * rows), 2 * rows)
            for j in range(cols):
                base = t * block + j * rows
                kv = jnp.concatenate([part[base : base + rows] for part in parts], axis=0).astype(BF16)
                k_scr[j, dest, :] = kv[:, :C]
                v_scr[j, dest, :] = kv[:, C:]
        return 0

    lax.fori_loop(0, pairs // batch, make_kv, 0)

    normed = normed_ref[...]
    queries = mm(normed, w_in_ref[:, :C])
    gate_raw = mm(normed, w_in_ref[:, 3 * C :])
    key_bias = (mask_ref[...].astype(F32) - 1.0) * 1000000000.0

    def head_mask(h):
        lane = lax.broadcasted_iota(jnp.int32, (rows, C), 1)
        return (lane >= h * DH) & (lane < (h + 1) * DH)

    def stack(x):
        return jnp.concatenate([jnp.where(head_mask(h), x, 0.0) for h in range(H)], axis=0)

    def unstack(x):
        out = jnp.where(head_mask(0), x[:rows], 0.0)
        for h in range(1, H):
            out = jnp.where(head_mask(h), x[h * rows : (h + 1) * rows], out)
        return out

    q_stack = [stack(queries[j * rows : (j + 1) * rows]) for j in range(cols)]
    for j in range(cols):
        s_scr[j] = mm_t(q_stack[j].astype(BF16), k_scr[j])

    def soft(r, _):
        at = pl.ds(pl.multiple_of(r * STEP, STEP), STEP)
        bias = bias_ref[at, :]
        for j in range(cols):
            s = s_scr[j, at, :] * SCALE + bias + key_bias
            e = jnp.exp(s - jnp.max(s, axis=-1, keepdims=True))
            e_scr[j, at, :] = e.astype(BF16)
            sum_scr[j, at, :] = jnp.broadcast_to(jnp.sum(e, axis=-1, keepdims=True), (STEP, C))
        return 0

    lax.fori_loop(0, H * rows // STEP, soft, 0, unroll=UNROLL)
    inv = [1.0 / sum_scr[j] for j in range(cols)]
    o_stack = [mm(e_scr[j], v_scr[j]) * inv[j] for j in range(cols)]
    heads_out = jnp.concatenate([unstack(o) for o in o_stack], axis=0)

    open_ = jax.nn.sigmoid(gate_raw)
    source, cot = both_ref[:block, :], both_ref[block:, :]
    gated = (heads_out * open_).astype(BF16)
    mid = source + mm(gated, w_out_ref[...])
    mid_hat, mid_rstd = center(mid)
    gain = gain_ref[...]
    pre = mm((mid_hat * gain).astype(BF16), w_up_ref[...])
    gs = jax.nn.sigmoid(pre)
    slope = gs + pre * gs * (1.0 - gs)
    d_hidden = (mm_t(cot.astype(BF16), w_down_ref[...]) * slope).astype(BF16)
    d_trans = mm_t(d_hidden, w_up_ref[...])
    d_mid = cot + center_back(mid_hat, mid_rstd, gain, d_trans)
    d_gated = mm_t(d_mid.astype(BF16), w_out_ref[...])
    d_heads = d_gated * open_
    d_gate = d_gated * heads_out * open_ * (1.0 - open_)
    loc_ref[:block, :] = d_mid

    w_kv = w_in_ref[:, C : 3 * C]
    d_query, do_t = [], []
    for j in range(cols):
        do_f = stack(d_heads[j * rows : (j + 1) * rows]).astype(BF16).astype(F32) * inv[j]
        do_stack = do_f.astype(BF16)
        do_t.append(do_f.T.astype(BF16))
        dot_row = jnp.sum(o_stack[j] * do_stack.astype(F32), axis=-1, keepdims=True)
        sum_scr[j] = jnp.broadcast_to(dot_row, (H * rows, C))
        s_scr[j] = mm_t(do_stack, v_scr[j])

    def back(r, _):
        at = pl.ds(pl.multiple_of(r * STEP, STEP), STEP)
        total = None
        for j in range(cols):
            ds = e_scr[j, at, :].astype(F32) * (s_scr[j, at, :] - sum_scr[j, at, :1])
            dsb_scr[j, at, :] = ds.astype(BF16)
            total = ds if total is None else total + ds
        ds_scr[at, :] = total
        return 0

    lax.fori_loop(0, H * rows // STEP, back, 0, unroll=UNROLL)
    lane = lax.broadcasted_iota(jnp.int32, (rows, C), 1)

    def put_db(t, _):
        at = pl.ds(pl.multiple_of(t * C, C), C)
        xs = [ds_scr[pl.ds(h * rows, rows), at] for h in range(H)]
        low, even = (lane & 64) == 0, (lane & 32) == 0
        ys = [None] * H
        for h in range(2):
            ys[h] = jnp.where(low, xs[h], pltpu.roll(xs[h + 2], 64, 1))
            ys[h + 2] = jnp.where(low, pltpu.roll(xs[h], 64, 1), xs[h + 2])
        groups = []
        for h in (0, 2):
            groups.append(jnp.where(even, ys[h], pltpu.roll(ys[h + 1], 32, 1)))
            groups.append(jnp.where(even, pltpu.roll(ys[h], 96, 1), ys[h + 1]))
        start = pl.multiple_of(t * 4 * rows, 4 * rows)
        db_ref[pl.ds(start, 4 * rows), :] = jnp.concatenate(groups, axis=0).astype(BF16)
        return 0

    lax.fori_loop(0, n // C, put_db, 0, unroll=UDB)
    copies[0].start()

    for j in range(cols):
        ds_b = dsb_scr[j]
        d_query.append(unstack(mm(ds_b, k_scr[j])) * SCALE)
        dk = mm(q_stack[j].T.astype(BF16), ds_b) * SCALE
        dv = mm(do_t[j], e_scr[j])
        dn_scr[j] = mm(w_kv, jnp.concatenate([dk, dv], axis=0).astype(BF16)).T

    hi, lo = halves(jnp.concatenate([jnp.concatenate(d_query, axis=0), d_gate], axis=1))
    w_qg = jnp.concatenate([w_in_ref[:, :C], w_in_ref[:, 3 * C :]], axis=1)
    loc_ref[block:, :] = mm_t(hi, w_qg) + mm_t(lo, w_qg)
    copies[3].start()

    chip = lax.div(lax.axis_index("ctx"), 2)
    for place in range(pairs):
        p = lax.bitwise_xor(chip, relative(place))
        for ref, which in ((keep_ref, core), (send_ref, 1 - core)):
            at = pl.ds(pl.multiple_of((2 * p + which) * rows, rows), rows)
            both = jnp.concatenate([dn_scr[j, at, :] for j in range(cols)], axis=0)
            ref[place * block : (place + 1) * block, :] = both.astype(ref.dtype)

    copies[1].start()
    copies[2].start()
    for copy in copies:
        copy.wait()


def quarter_kernel(keep_ref, *refs):
    parts, (kept_ref, *sent) = refs[: -4], refs[-4 :]
    size = kept_ref.shape[0]
    for q in range(4):
        at = slice(q * size, (q + 1) * size)
        total = keep_ref[at, :]
        for part in parts:
            total = total + part[at, :].astype(F32)
        if q == 0:
            kept_ref[...] = total
        else:
            sent[q - 1][...] = total.astype(BF16)


def last_kernel(kept_ref, a_ref, b_ref, c_ref, loc_ref, both_ref, gain_ref, after_ref, out_ref):
    del after_ref
    half = loc_ref.shape[0] // 2
    total = loc_ref[half:, :] + kept_ref[...]
    for part in (a_ref, b_ref, c_ref):
        total = total + part[...].astype(F32)
    hat, rstd = center(both_ref[:half, :])
    d_pair = loc_ref[:half, :] + center_back(hat, rstd, gain_ref[...], total)
    local = half // 2 // (out_ref.shape[0] // 8)
    out, at = iotas(out_ref.shape[0], half)
    j, r, valid = split8(out, local)
    order = pick(valid & (at == j * (half // 2) + (out >> 3) * local + r))
    out_ref[...] = mm(order, d_pair.astype(BF16)).astype(BF16)


def finish_kernel(x_ref, out_ref):
    local, n_cols, _ = out_ref.shape
    out, at = iotas(local * n_cols, x_ref.shape[0])
    j, r, valid = split8(at, local)
    order = pick(valid & (out == r * n_cols + (at >> 3) * 2 + j))
    out_ref[...] = mm(order, x_ref[...]).reshape(out_ref.shape)


def bias_kernel(parts_ref, out_ref):
    rows = out_ref.shape[1]
    total = parts_ref[0].astype(F32)
    for p in range(1, parts_ref.shape[0]):
        total = total + parts_ref[p].astype(F32)
    for h in range(H):
        out_ref[h] = jnp.concatenate(
            [total[t * rows : (t + 1) * rows, h * DH : (h + 1) * DH] for t in range(3)], axis=1
        )


def call(kernel, out_shape, limit=16, n_in=None, unread=0):
    specs = {}
    if unread:
        vmem = pl.BlockSpec(memory_space=pltpu.VMEM)
        specs["in_specs"] = [vmem] * (n_in - unread) + [pl.BlockSpec(memory_space=pl.ANY)] * unread
    return pl.pallas_call(
        kernel,
        out_shape=out_shape,
        **specs,
        compiler_params=pltpu.CompilerParams(vmem_limit_bytes=limit * 1024 * 1024),
    )


def run_main(mine, other, normed, both, bias, mask, *weights):
    cols, n = 2, bias.shape[1]
    rows = bias.shape[0] // H
    block = cols * rows
    outs = (
        ((n // DH * rows, C), BF16),
        ((n * cols // 2, C), F32),
        ((n * cols // 2, C), BF16),
        ((2 * block, C), F32),
    )
    scratch = [pltpu.VMEM(shape, dtype) for shape, dtype in outs]
    scratch += [pltpu.SemaphoreType.DMA((len(outs),))]
    scratch += [
        pltpu.VMEM((cols, n, C), BF16),
        pltpu.VMEM((cols, n, C), BF16),
        pltpu.VMEM((cols, H * rows, n), F32),
        pltpu.VMEM((cols, H * rows, n), BF16),
        pltpu.VMEM((cols, H * rows, C), F32),
        pltpu.VMEM((H * rows, n), F32),
        pltpu.VMEM((cols, H * rows, n), BF16),
        pltpu.VMEM((cols, n, C), F32),
    ]
    return pl.pallas_call(
        main_kernel,
        out_shape=[jax.ShapeDtypeStruct(shape, dtype) for shape, dtype in outs],
        out_specs=[pl.BlockSpec(memory_space=pltpu.HBM)] * len(outs),
        scratch_shapes=scratch,
        compiler_params=pltpu.CompilerParams(vmem_limit_bytes=LIMIT * 1024 * 1024),
    )(mine, other, normed, both, bias, mask, *weights)


def per_device(pair, cotangent, residue_mask, bias, ln_attend, w_in, w_out, ln_trans, w_up, w_down):
    n_dap = lax.axis_size("dap")
    n_ctx = lax.axis_size("ctx")
    local, n_cols, _ = pair.shape
    cols = n_cols // n_dap
    rows = local * n_dap
    n = rows * n_ctx
    block = cols * rows

    x = call(first_kernel, jax.ShapeDtypeStruct((n_dap * 16, C), BF16))(pair, cotangent)
    x = lax.all_to_all(x, "dap", 0, 0, tiled=True)
    normed, both = call(
        prep_kernel,
        (jax.ShapeDtypeStruct((block, C), BF16), jax.ShapeDtypeStruct((2 * block, C), F32)),
    )(x, ln_attend[None])

    gathered = jnp.broadcast_to(normed[None], (n_ctx // 2, block, C)).reshape(n_ctx // 2 * block, C)
    gathered = lax.all_to_all(gathered, "ctx", 0, 0, tiled=True, axis_index_groups=CHIPS)
    other = lax.ppermute(gathered, "ctx", [(i, i ^ 1) for i in range(n_ctx)])

    db, keep, send, loc = run_main(
        gathered, other, normed, both, bias.reshape(H * rows, n), residue_mask[None], w_in, w_out, ln_trans[None],
        w_up, w_down,
    )
    db = lax.all_to_all(db, "dap", 0, 0, tiled=True).reshape(n_dap, n // n_dap // DH * rows, C)

    parts = [lax.ppermute(send, "ctx", [(i, i ^ 1) for i in range(n_ctx)])]
    for flips in FLIPS:
        size = keep.shape[0] // 4
        shapes = [jax.ShapeDtypeStruct((size, C), dtype) for dtype in (F32, BF16, BF16, BF16)]
        keep, *sent = call(quarter_kernel, shapes)(keep, *parts)
        parts = [lax.ppermute(part, "ctx", [(i, i ^ flip) for i in range(n_ctx)]) for part, flip in zip(sent, flips)]

    d_pair = call(last_kernel, jax.ShapeDtypeStruct((n_dap * 8, C), BF16), n_in=8, unread=1)(
        keep, *parts, loc, both, ln_attend[None], db
    )
    bias_grad = call(bias_kernel, jax.ShapeDtypeStruct((H, rows, n // n_dap), F32))(db)
    d_pair = lax.all_to_all(d_pair, "dap", 0, 0, tiled=True)
    pair_grad = call(finish_kernel, jax.ShapeDtypeStruct((local, n_cols, C), F32))(d_pair)
    return (pair_grad, bias_grad)


def solution(mesh):
    in_specs = (
        P(("ctx", "dap"), None, None),
        P(("ctx", "dap"), None, None),
        P(),
        P(None, "ctx", None),
        P(),
        P(),
        P(),
        P(),
        P(),
        P(),
    )
    out_specs = (P(("ctx", "dap"), None, None), P(None, "ctx", "dap"))
    return jax.shard_map(
        per_device, mesh=mesh, in_specs=in_specs, out_specs=out_specs, check_vma=False
    )
```

time: 159 us -> 149 us (0.937)
  starting transfers between devices: 30 us -> 43.1 us
  waiting for transfers between devices: 42 us -> 30.5 us
  local copies, waits for them, and re-layouts: 8.77 us -> 4.09 us
  other arithmetic: 4.31 us -> 0 us
  Pallas kernels: 16.4 us -> 14.8 us
    ppermute x5 -> x7, waiting for transfers between devices: 31.9 us -> 12.8 us  [the longest x6 10.8 us: per_device(): lax.ppermute(part, 'ctx', [(i, i ^ flip) for i in range(n_ctx)])]
    ppermute x5 -> x7, starting transfers between devices: 11.5 us -> 26.7 us  [the longest x6 24.7 us: per_device(): lax.ppermute(part, 'ctx', [(i, i ^ flip) for i in range(n_ctx)])]
    all_to_all x1, waiting for transfers between devices: 0.01 us -> 6.73 us  [per_device(): lax.all_to_all(db, 'dap', 0, 0, tiled=True)]
    add x5 -> x0, other arithmetic: 3.37 us -> none  [the longest x1 2.19 us: per_device(): keep + lax.ppermute(send, 'ctx', [(i, i ^ 1) for i in range(n_ctx)]).asty...]
    all_to_all x1, starting transfers between devices: 10.6 us -> 8.6 us  [per_device(): d_pair = lax.all_to_all(d_pair, 'dap', 0, 0, tiled=True)]
    convert_element_type x5 -> x0, local copies, waits for them, and re-layouts: 1.83 us -> none  [the longest x4 1.15 us: per_device(): sent = lax.dynamic_index_in_dim(total, 1 - bit, 0, False).astype(BF16)]
    pallas_call x2 -> x6, Pallas kernels: 15.1 us -> 13.5 us  [the longest x1 11.2 us: run_main(): pl.pallas_call(main_kernel, out_shape=[jax.ShapeDtypeStruct(shape, dtype)...]
    unnamed x30 -> x22, local copies, waits for them, and re-layouts: 5.44 us -> 4 us
  transfers between devices with their start and end apart: 8 -> 10, of which waited for: 7 -> 6; matrix products, arithmetic and copies ran while one was open for 3% -> 0% of each run, Pallas kernels for 1% -> 1%
where the time goes in v3:
time: 149 us; the launch traced here: 148 us
  blocking collectives  54.9 us (37%)
  starting transfers between devices  43.1 us (29%)
  waiting for transfers between devices  30.5 us (20%)
  Pallas kernels  14.8 us (10%)
  local copies, waits for them, and re-layouts  4.09 us (3%)
    all_to_all x1, blocking collectives, per_device(): lax.all_to_all(gathered, 'ctx', 0, 0, tiled=True, axis_index_groups=CHIPS)  28.1 us
    all_to_all x1, blocking collectives, per_device(): x = lax.all_to_all(x, 'dap', 0, 0, tiled=True)  26.8 us
    ppermute x6, starting transfers between devices, per_device(): lax.ppermute(part, 'ctx', [(i, i ^ flip) for i in range(n_ctx)])  24.7 us
    pallas_call x1, Pallas kernels, run_main(): pl.pallas_call(main_kernel, out_shape=[jax.ShapeDtypeStruct(shape, dtype)...  11.2 us
    ppermute x6, waiting for transfers between devices, per_device(): lax.ppermute(part, 'ctx', [(i, i ^ flip) for i in range(n_ctx)])  10.8 us
    all_to_all x1, waiting for transfers between devices, per_device(): d_pair = lax.all_to_all(d_pair, 'dap', 0, 0, tiled=True)  9.03 us
    all_to_all x1, starting transfers between devices, per_device(): d_pair = lax.all_to_all(d_pair, 'dap', 0, 0, tiled=True)  8.6 us
    all_to_all x1, waiting for transfers between devices, per_device(): lax.all_to_all(db, 'dap', 0, 0, tiled=True)  6.73 us
  transfers between devices with their start and end apart: 10, of which 6 were waited for; matrix products, arithmetic and copies ran while one was open for 0% of the time, Pallas kernels for 1%

profile of v3, /device:TPU:2, one launch (start us, length us, event | category | flops | bytes accessed | tf_op | source)
XLA Modules:
  0.0 148.2 jit_solution(17854349865092335220)
XLA Ops:
  0.6 0.0 copy-start.1
  0.6 0.0 copy-start.2
  0.7 0.0 copy-start.4
  0.7 0.8 copy-done.4
  1.5 0.0 copy-start.5
  1.5 0.8 copy-done.5
  2.2 0.3 shard_map.113
  2.5 26.8 %all_to_all.39 = bf16[24,16,128]{2,1,0:T(8,128)(2,1)S(1)} all-to-all(bf16[24,16,128]{2,1,0:T(8,128)(2,1)S(1)} %bitcast.13), channel_id=1, replica_groups=mesh['dap'=24,'ctx'=32] {'dap'}, dimensions={0} | all-to-all | bytes 196608 | tf_op jit(solution)/shard_map/all_to_all | solution.py:352
  29.4 0.7 copy-done.7
  30.0 0.4 shard_map.114
  30.4 0.1 broadcast_in_dim.17
  30.5 28.1 %all_to_all.40 = bf16[16,144,128]{2,1,0:T(8,128)(2,1)S(1)} all-to-all(bf16[16,144,128]{2,1,0:T(8,128)(2,1)S(1)} %broadcast_in_dim.17), channel_id=1, replica_groups={{0,2,4,6,8,10,12,14,16,18,20,22,24,26,28,30},{1,3,5,7,9,11,13,15,17,19,..., dimensions={0} | all-to-all | bytes 1179648 | tf_op jit(solution)/shard_map/all_to_all | solution.py:359
  58.6 1.9 %collective-permute-start = (bf16[2304,128]{1,0:T(8,128)(2,1)S(1)}, bf16[2304,128]{1,0:T(8,128)(2,1)S(1)}, u32[]{:S(2)}, u32[]{:S(2)}) collective-permute-start(bf16[2304,128]{1,0:T(8,128)(2,1)S(1)} %bitcast.10), channel_id=1, source_target_pairs={{0,1},{1,0},{2,3},{3,2},{4,5},{5,4},{6,7},{7,6},{8,9},{9,8},{10,11... | collective-permute-start | bytes 1769480 | tf_op jit(solution)/shard_map/ppermute | solution.py:360
  60.5 0.0 copy-done.10
  60.5 1.9 %collective-permute-done.other_ref = bf16[2304,128]{1,0:T(8,128)(2,1)S(1)} collective-permute-done((bf16[2304,128]{1,0:T(8,128)(2,1)S(1)}, bf16[2304,128]{1,0:T(8,128)(2,1)S(1)}, u32[]{:S(2)}, u32[]{:S(2)}) %collective-permute-start) | collective-permute-done | bytes 589856 | tf_op jit(solution)/shard_map/ppermute | solution.py:360
  62.5 0.0 copy-done.1
  62.5 0.0 copy-done.2
  62.5 0.0 copy-done.3
  62.5 0.0 copy-done.6
  62.5 0.0 copy-done.9
  62.5 0.0 copy-start
  62.5 1.7 %copy-done = f32[4,72,2304]{2,1,0:T(8,128)S(1)} copy-done((f32[4,72,2304]{2,1,0:T(8,128)S(1)}, f32[4,72,2304]{2,1,0:T(8,128)}, u32[]{:S(2)}) %copy-start) | copy-done | bytes 2654232
  64.3 11.2 %shard_map.115 = (bf16[5184,128]{1,0:T(8,128)(2,1)}, f32[2304,128]{1,0:T(8,128)S(1)}, bf16[2304,128]{1,0:T(8,128)(2,1)S(1)}, f32[288,128]{1,0:T(8,128)S(1)}) custom-call(bf16[2304,128]{1,0:T(8,128)(2,1)S(1)} %bitcast.11, bf16[2304,128]{1,0:T(8,128)(2,1)S(1)} %collective-permute-done.other_ref, bf16[144,128]{1,0:T(8,128)(2,1)S(1)} %get-tuple-element.16.normed_ref, ...), custom_call_target="tpu_custom_call" | custom-call | tf_op jit(solution)/shard_map/pallas_call | solution.py:333
  75.5 5.9 %all-to-all-start.2 = ((bf16[24,216,128]{2,1,0:T(8,128)(2,1)}), bf16[24,216,128]{2,1,0:T(8,128)(2,1)S(1)}, u32[]{:S(2)}, u32[]{:S(2)}) async-start(bf16[24,216,128]{2,1,0:T(8,128)(2,1)} %bitcast.6), calls=%async_computation.2 | async-start | bytes 2654208 | tf_op jit(solution)/shard_map/all_to_all | solution.py:366
  81.4 0.0 copy-start.8
  81.4 1.9 %collective-permute-start.1 = (bf16[2304,128]{1,0:T(8,128)(2,1)S(1)}, bf16[2304,128]{1,0:T(8,128)(2,1)S(1)}, u32[]{:S(2)}, u32[]{:S(2)}) collective-permute-start(bf16[2304,128]{1,0:T(8,128)(2,1)S(1)} %get-tuple-element.19), channel_id=1, source_target_pairs={{0,1},{1,0},{2,3},{3,2},{4,5},{5,4},{6,7},{7,6},{8,9},{9,8},{10,11... | collective-permute-start | bytes 1769480 | tf_op jit(solution)/shard_map/ppermute | solution.py:368
  83.3 2.0 %collective-permute-done.1.refs_0_ = bf16[2304,128]{1,0:T(8,128)(2,1)S(1)} collective-permute-done((bf16[2304,128]{1,0:T(8,128)(2,1)S(1)}, bf16[2304,128]{1,0:T(8,128)(2,1)S(1)}, u32[]{:S(2)}, u32[]{:S(2)}) %collective-permute-start.1) | collective-permute-done | bytes 589856 | tf_op jit(solution)/shard_map/ppermute | solution.py:368
  85.3 0.1 shard_map.116
  85.4 2.4 %collective-permute-start.2 = (bf16[576,128]{1,0:T(8,128)(2,1)S(1)}, bf16[576,128]{1,0:T(8,128)(2,1)S(1)}, u32[]{:S(2)}, u32[]{:S(2)}) collective-permute-start(bf16[576,128]{1,0:T(8,128)(2,1)S(1)} %get-tuple-element.21), channel_id=1, source_target_pairs={{0,4},{1,5},{2,6},{3,7},{4,0},{5,1},{6,2},{7,3},{8,12},{9,13},{10,... | collective-permute-start | bytes 442376 | tf_op jit(solution)/shard_map/ppermute | solution.py:373
  87.8 2.7 %collective-permute-start.3 = (bf16[576,128]{1,0:T(8,128)(2,1)S(1)}, bf16[576,128]{1,0:T(8,128)(2,1)S(1)}, u32[]{:S(2)}, u32[]{:S(2)}) collective-permute-start(bf16[576,128]{1,0:T(8,128)(2,1)S(1)} %get-tuple-element.22), channel_id=1, source_target_pairs={{0,8},{1,9},{2,10},{3,11},{4,12},{5,13},{6,14},{7,15},{8,0},{9,1},... | collective-permute-start | bytes 442376 | tf_op jit(solution)/shard_map/ppermute | solution.py:373
  90.5 5.0 %collective-permute-start.4 = (bf16[576,128]{1,0:T(8,128)(2,1)S(1)}, bf16[576,128]{1,0:T(8,128)(2,1)S(1)}, u32[]{:S(2)}, u32[]{:S(2)}) collective-permute-start(bf16[576,128]{1,0:T(8,128)(2,1)S(1)} %get-tuple-element.23), channel_id=1, source_target_pairs={{0,12},{1,13},{2,14},{3,15},{4,8},{5,9},{6,10},{7,11},{8,4},{9,5},... | collective-permute-start | bytes 442376 | tf_op jit(solution)/shard_map/ppermute | solution.py:373
  95.5 0.0 collective-permute-done.2.refs_0_
  95.5 8.1 %collective-permute-done.3.refs_1_ = bf16[576,128]{1,0:T(8,128)(2,1)S(1)} collective-permute-done((bf16[576,128]{1,0:T(8,128)(2,1)S(1)}, bf16[576,128]{1,0:T(8,128)(2,1)S(1)}, u32[]{:S(2)}, u32[]{:S(2)}) %collective-permute-start.3) | collective-permute-done | bytes 147488 | tf_op jit(solution)/shard_map/ppermute | solution.py:373
  103.6 0.0 collective-permute-done.4.refs_2_
  103.6 0.1 shard_map.117
  103.7 1.9 %collective-permute-start.5 = (bf16[144,128]{1,0:T(8,128)(2,1)S(1)}, bf16[144,128]{1,0:T(8,128)(2,1)S(1)}, u32[]{:S(2)}, u32[]{:S(2)}) collective-permute-start(bf16[144,128]{1,0:T(8,128)(2,1)S(1)} %get-tuple-element.25), channel_id=1, source_target_pairs={{0,2},{1,3},{2,0},{3,1},{4,6},{5,7},{6,4},{7,5},{8,10},{9,11},{10,... | collective-permute-start | bytes 110600 | tf_op jit(solution)/shard_map/ppermute | solution.py:373
  105.6 3.1 %collective-permute-start.6 = (bf16[144,128]{1,0:T(8,128)(2,1)S(1)}, bf16[144,128]{1,0:T(8,128)(2,1)S(1)}, u32[]{:S(2)}, u32[]{:S(2)}) collective-permute-start(bf16[144,128]{1,0:T(8,128)(2,1)S(1)} %get-tuple-element.26), channel_id=1, source_target_pairs={{0,16},{1,17},{2,18},{3,19},{4,20},{5,21},{6,22},{7,23},{8,24},{9,... | collective-permute-start | bytes 110600 | tf_op jit(solution)/shard_map/ppermute | solution.py:373
  108.7 9.6 %collective-permute-start.7 = (bf16[144,128]{1,0:T(8,128)(2,1)S(1)}, bf16[144,128]{1,0:T(8,128)(2,1)S(1)}, u32[]{:S(2)}, u32[]{:S(2)}) collective-permute-start(bf16[144,128]{1,0:T(8,128)(2,1)S(1)} %get-tuple-element.27), channel_id=1, source_target_pairs={{0,18},{1,19},{2,16},{3,17},{4,22},{5,23},{6,20},{7,21},{8,26},{9,... | collective-permute-start | bytes 110600 | tf_op jit(solution)/shard_map/ppermute | solution.py:373
  118.3 0.0 collective-permute-done.5.a_ref
  118.3 0.0 collective-permute-done.6.b_ref
  118.3 2.7 %collective-permute-done.7.c_ref = bf16[144,128]{1,0:T(8,128)(2,1)S(1)} collective-permute-done((bf16[144,128]{1,0:T(8,128)(2,1)S(1)}, bf16[144,128]{1,0:T(8,128)(2,1)S(1)}, u32[]{:S(2)}, u32[]{:S(2)}) %collective-permute-start.7) | collective-permute-done | bytes 36896 | tf_op jit(solution)/shard_map/ppermute | solution.py:373
  121.1 6.7 %all-to-all-done.2.after_ref.parts_ref = bf16[24,216,128]{2,1,0:T(8,128)(2,1)S(1)} async-done(((bf16[24,216,128]{2,1,0:T(8,128)(2,1)}), bf16[24,216,128]{2,1,0:T(8,128)(2,1)S(1)}, u32[]{:S(2)}, u32[]{:S(2)}) %all-to-all-start.2) | async-done | bytes 1327136 | tf_op jit(solution)/shard_map/all_to_all | solution.py:366
  127.8 0.0 copy-done.8
  127.8 1.0 shard_map.118
  128.8 8.6 %all-to-all-start.3 = ((bf16[24,8,128]{2,1,0:T(8,128)(2,1)}), bf16[24,8,128]{2,1,0:T(8,128)(2,1)S(1)}, u32[]{:S(2)}, u32[]{:S(2)}) async-start(bf16[24,8,128]{2,1,0:T(8,128)(2,1)} %bitcast.7), calls=%async_computation.3 | async-start | bytes 98304 | tf_op jit(solution)/shard_map/all_to_all | solution.py:379
  137.4 1.0 shard_map.120
  138.4 9.0 %all-to-all-done.3 = bf16[24,8,128]{2,1,0:T(8,128)(2,1)S(1)} async-done(((bf16[24,8,128]{2,1,0:T(8,128)(2,1)}), bf16[24,8,128]{2,1,0:T(8,128)(2,1)S(1)}, u32[]{:S(2)}, u32[]{:S(2)}) %all-to-all-start.3) | async-done | bytes 49184 | tf_op jit(solution)/shard_map/all_to_all | solution.py:379
  147.4 0.8 shard_map.119
  (6 shorter events, 0.0 us)
Async XLA Ops:
  0.6 61.8 %copy-start.1 = (bf16[128,512]{1,0:T(8,128)(2,1)S(1)}, bf16[128,512]{1,0:T(8,128)(2,1)}, u32[]{:S(2)}) copy-start(bf16[128,512]{1,0:T(8,128)(2,1)} %w_in_ref.1) | copy-start | bytes 393220
  0.6 61.8 %copy-start.2 = (bf16[128,512]{1,0:T(8,128)(2,1)S(1)}, bf16[128,512]{1,0:T(8,128)(2,1)}, u32[]{:S(2)}) copy-start(bf16[128,512]{1,0:T(8,128)(2,1)} %w_up_ref.1) | copy-start | bytes 393220
  0.7 0.8 copy-start.4
  1.5 0.8 copy-start.5
  2.2 60.2 %copy-start.3 = (bf16[512,128]{1,0:T(8,128)(2,1)S(1)}, bf16[512,128]{1,0:T(8,128)(2,1)}, u32[]{:S(2)}) copy-start(bf16[512,128]{1,0:T(8,128)(2,1)} %w_down_ref.1) | copy-start | bytes 393220
  2.2 60.2 %copy-start.6 = (bf16[128,128]{1,0:T(8,128)(2,1)S(1)}, bf16[128,128]{1,0:T(8,128)(2,1)}, u32[]{:S(2)}) copy-start(bf16[128,128]{1,0:T(8,128)(2,1)} %w_out_ref.1) | copy-start | bytes 98308
  29.4 0.7 copy-start.7
  30.0 30.5 %copy-start.10 = (s32[2304]{0:T(1024)S(1)}, s32[2304]{0:T(1024)}, u32[]{:S(2)}) copy-start(s32[2304]{0:T(1024)} %param.12) | copy-start | bytes 27652
  30.0 32.4 %copy-start.9 = (f32[128]{0:T(128)S(1)}, f32[128]{0:T(128)}, u32[]{:S(2)}) copy-start(f32[128]{0:T(128)} %param.17) | copy-start | bytes 1540
  58.6 3.9 %collective-permute-start = (bf16[2304,128]{1,0:T(8,128)(2,1)S(1)}, bf16[2304,128]{1,0:T(8,128)(2,1)S(1)}, u32[]{:S(2)}, u32[]{:S(2)}) collective-permute-start(bf16[2304,128]{1,0:T(8,128)(2,1)S(1)} %bitcast.10), channel_id=1, source_target_pairs={{0,1},{1,0},{2,3},{3,2},{4,5},{5,4},{6,7},{7,6},{8,9},{9,8},{10,11... | collective-permute-start | bytes 1769480 | tf_op jit(solution)/shard_map/ppermute | solution.py:360
  62.5 1.8 %copy-start = (f32[4,72,2304]{2,1,0:T(8,128)S(1)}, f32[4,72,2304]{2,1,0:T(8,128)}, u32[]{:S(2)}) copy-start(f32[4,72,2304]{2,1,0:T(8,128)} %param.13) | copy-start | bytes 7962628
  75.5 52.3 %all-to-all-start.2 = ((bf16[24,216,128]{2,1,0:T(8,128)(2,1)}), bf16[24,216,128]{2,1,0:T(8,128)(2,1)S(1)}, u32[]{:S(2)}, u32[]{:S(2)}) async-start(bf16[24,216,128]{2,1,0:T(8,128)(2,1)} %bitcast.6), calls=%async_computation.2 | async-start | bytes 2654208 | tf_op jit(solution)/shard_map/all_to_all | solution.py:366
  81.4 46.4 %copy-start.8 = (f32[128]{0:T(128)S(1)}, f32[128]{0:T(128)}, u32[]{:S(2)}) copy-start(f32[128]{0:T(128)} %param.14) | copy-start | bytes 1540
  81.4 3.9 %collective-permute-start.1 = (bf16[2304,128]{1,0:T(8,128)(2,1)S(1)}, bf16[2304,128]{1,0:T(8,128)(2,1)S(1)}, u32[]{:S(2)}, u32[]{:S(2)}) collective-permute-start(bf16[2304,128]{1,0:T(8,128)(2,1)S(1)} %get-tuple-element.19), channel_id=1, source_target_pairs={{0,1},{1,0},{2,3},{3,2},{4,5},{5,4},{6,7},{7,6},{8,9},{9,8},{10,11... | collective-permute-start | bytes 1769480 | tf_op jit(solution)/shard_map/ppermute | solution.py:368
  85.4 10.1 %collective-permute-start.2 = (bf16[576,128]{1,0:T(8,128)(2,1)S(1)}, bf16[576,128]{1,0:T(8,128)(2,1)S(1)}, u32[]{:S(2)}, u32[]{:S(2)}) collective-permute-start(bf16[576,128]{1,0:T(8,128)(2,1)S(1)} %get-tuple-element.21), channel_id=1, source_target_pairs={{0,4},{1,5},{2,6},{3,7},{4,0},{5,1},{6,2},{7,3},{8,12},{9,13},{10,... | collective-permute-start | bytes 442376 | tf_op jit(solution)/shard_map/ppermute | solution.py:373
  87.8 15.8 %collective-permute-start.3 = (bf16[576,128]{1,0:T(8,128)(2,1)S(1)}, bf16[576,128]{1,0:T(8,128)(2,1)S(1)}, u32[]{:S(2)}, u32[]{:S(2)}) collective-permute-start(bf16[576,128]{1,0:T(8,128)(2,1)S(1)} %get-tuple-element.22), channel_id=1, source_target_pairs={{0,8},{1,9},{2,10},{3,11},{4,12},{5,13},{6,14},{7,15},{8,0},{9,1},... | collective-permute-start | bytes 442376 | tf_op jit(solution)/shard_map/ppermute | solution.py:373
  90.5 13.1 %collective-permute-start.4 = (bf16[576,128]{1,0:T(8,128)(2,1)S(1)}, bf16[576,128]{1,0:T(8,128)(2,1)S(1)}, u32[]{:S(2)}, u32[]{:S(2)}) collective-permute-start(bf16[576,128]{1,0:T(8,128)(2,1)S(1)} %get-tuple-element.23), channel_id=1, source_target_pairs={{0,12},{1,13},{2,14},{3,15},{4,8},{5,9},{6,10},{7,11},{8,4},{9,5},... | collective-permute-start | bytes 442376 | tf_op jit(solution)/shard_map/ppermute | solution.py:373
  103.7 14.7 %collective-permute-start.5 = (bf16[144,128]{1,0:T(8,128)(2,1)S(1)}, bf16[144,128]{1,0:T(8,128)(2,1)S(1)}, u32[]{:S(2)}, u32[]{:S(2)}) collective-permute-start(bf16[144,128]{1,0:T(8,128)(2,1)S(1)} %get-tuple-element.25), channel_id=1, source_target_pairs={{0,2},{1,3},{2,0},{3,1},{4,6},{5,7},{6,4},{7,5},{8,10},{9,11},{10,... | collective-permute-start | bytes 110600 | tf_op jit(solution)/shard_map/ppermute | solution.py:373
  105.6 12.7 %collective-permute-start.6 = (bf16[144,128]{1,0:T(8,128)(2,1)S(1)}, bf16[144,128]{1,0:T(8,128)(2,1)S(1)}, u32[]{:S(2)}, u32[]{:S(2)}) collective-permute-start(bf16[144,128]{1,0:T(8,128)(2,1)S(1)} %get-tuple-element.26), channel_id=1, source_target_pairs={{0,16},{1,17},{2,18},{3,19},{4,20},{5,21},{6,22},{7,23},{8,24},{9,... | collective-permute-start | bytes 110600 | tf_op jit(solution)/shard_map/ppermute | solution.py:373
  108.7 12.3 %collective-permute-start.7 = (bf16[144,128]{1,0:T(8,128)(2,1)S(1)}, bf16[144,128]{1,0:T(8,128)(2,1)S(1)}, u32[]{:S(2)}, u32[]{:S(2)}) collective-permute-start(bf16[144,128]{1,0:T(8,128)(2,1)S(1)} %get-tuple-element.27), channel_id=1, source_target_pairs={{0,18},{1,19},{2,16},{3,17},{4,22},{5,23},{6,20},{7,21},{8,26},{9,... | collective-permute-start | bytes 110600 | tf_op jit(solution)/shard_map/ppermute | solution.py:373
  128.8 18.6 %all-to-all-start.3 = ((bf16[24,8,128]{2,1,0:T(8,128)(2,1)}), bf16[24,8,128]{2,1,0:T(8,128)(2,1)S(1)}, u32[]{:S(2)}, u32[]{:S(2)}) async-start(bf16[24,8,128]{2,1,0:T(8,128)(2,1)} %bitcast.7), calls=%async_computation.3 | async-start | bytes 98304 | tf_op jit(solution)/shard_map/all_to_all | solution.py:379
